TPU v7x, 128 devices: a whole 4x4x4 slice. The times are simulated.
128 devices in a mesh: dp: 32 (over x, z_hi, y), tensor: 4 (over z_lo, core).
Axes of the slice: x: 4, y: 4, z: 4 (z_hi: 2, z_lo: 2; z = z_hi * 2 + z_lo), core: 2. Of those that a mesh axis runs over, the one named last changes fastest.
Arguments:
- block_in: bfloat16 [16384, 1536], P(('dp', 'tensor')), may hold values from -6 to 6
- out_grad: bfloat16 [16384, 1536], P(('dp', 'tensor')), may hold values from -6 to 6
- condition: bfloat16 [96, 1024], P('dp'), may hold values from -6 to 6
- captions: bfloat16 [96, 256, 4096], P('dp'), may hold values from -6 to 6
- caption_len: int32 [96], P('dp'), may hold values from 64 to 256
- segment_ids: int32 [16384], P('dp'), may hold values from 0 to 2, as said below
- ada_weight: bfloat16 [1024, 6144], P(None, 'tensor'), may hold values from -0.1875 to 0.1875
- norm_gains: float32 [4, 1536], replicated, may hold values from 0.25 to 1.75
- query_weight: bfloat16 [1536, 1536], P(None, 'tensor'), may hold values from -0.15625 to 0.15625
- key_weight: bfloat16 [1536, 1536], P(None, 'tensor'), may hold values from -0.15625 to 0.15625
- value_weight: bfloat16 [1536, 1536], P(None, 'tensor'), may hold values from -0.15625 to 0.15625
- head_gains: float32 [3, 64], replicated, may hold values from 0.25 to 1.75
- textkey_weight: bfloat16 [4096, 1536], P(None, 'tensor'), may hold values from -0.09375 to 0.09375
- textvalue_weight: bfloat16 [4096, 1536], P(None, 'tensor'), may hold values from -0.09375 to 0.09375
- cross_gate: float32 [24], P('tensor'), may hold values from 0.3 to 1.5
- out_weight: bfloat16 [1536, 1536], P('tensor'), may hold values from -0.15625 to 0.15625
- gate_weight: bfloat16 [1536, 4096], P(None, 'tensor'), may hold values from -0.15625 to 0.15625
- up_weight: bfloat16 [1536, 4096], P(None, 'tensor'), may hold values from -0.15625 to 0.15625
- down_weight: bfloat16 [4096, 1536], P('tensor'), may hold values from -0.09375 to 0.09375
Outputs:
- block_out: bfloat16 [16384, 1536], P(('dp', 'tensor'))
- in_grad: bfloat16 [16384, 1536], P(('dp', 'tensor'))
- ada_grad: float32 [1024, 6144], P('dp', 'tensor')
- norm_grads: float32 [4, 1536], replicated
- query_grad: float32 [1536, 1536], P('dp', 'tensor')
- key_grad: float32 [1536, 1536], P('dp', 'tensor')
- value_grad: float32 [1536, 1536], P('dp', 'tensor')
- head_grads: float32 [3, 64], replicated
- textkey_grad: float32 [4096, 1536], P('dp', 'tensor')
- textvalue_grad: float32 [4096, 1536], P('dp', 'tensor')
- crossgate_grad: float32 [24], replicated
- outw_grad: float32 [1536, 1536], P('tensor', 'dp')
- gate_grad: float32 [1536, 4096], P('dp', 'tensor')
- up_grad: float32 [1536, 4096], P('dp', 'tensor')
- down_grad: float32 [4096, 1536], P('tensor', 'dp')
Inputs may be any that keep to these rules, and one draw needn't show every extreme that they name: `segment_ids`: within each sequence the ids never fall, every one of 0 to 2 holds one run of rows, and one segment is longer than 384.
All inputs are finite; a program needn't handle non-finite values.
Results may differ from a plain program's by a relative error of at most 0.025.
Values may be sent and summed in bfloat16 or wider, within the bound.
No kernel may reach another device: no remote copies, remote signals or barrier semaphores. Data moves between devices by JAX's collectives and lax.ppermute only.
A program may use at most 192 MiB of HBM per device.

v0:
```python
import math

import jax
import jax.numpy as jnp
from jax import lax
from jax.sharding import PartitionSpec as P

HEADS = 24
HEAD = 64
TXT = 256
SEGS = 3


EPS = 1e-06
PRECISION = lax.Precision.HIGHEST


def contract_rows(left, right):
    return lax.dot_general(
        left, right, (((0,), (0,)), ((), ())), preferred_element_type=jnp.float32
    )


def times_transpose(left, right):
    return lax.dot_general(
        left, right, (((1,), (1,)), ((), ())), preferred_element_type=jnp.float32
    )


def rms(values):
    return values * lax.rsqrt(jnp.mean(values * values, axis=-1, keepdims=True) + EPS)


def norm_mod(values, gain, scale):
    return rms(values) * gain * (1.0 + scale)


def residual_add(base, branch, gain, gate_rows):
    return base + jnp.tanh(gate_rows) * rms(branch) * gain


def head_norm(values, gain):
    return rms(values.reshape(values.shape[0], -1, HEAD)) * gain


def rotate(values, cosine, sine):
    half = HEAD // 2
    first = values[..., :half]
    second = values[..., half:]
    cosine = cosine[:, None, :]
    sine = sine[:, None, :]
    return jnp.concatenate(
        [first * cosine - second * sine, first * sine + second * cosine], axis=-1
    )


def rope_tables(segments):
    labels = jnp.arange(SEGS, dtype=jnp.int32)
    starts = jnp.sum((segments[None, :] < labels[:, None]).astype(jnp.int32), axis=1)
    member = (segments[:, None] == labels[None, :]).astype(jnp.int32)
    places = jnp.arange(segments.shape[0], dtype=jnp.int32) - jnp.sum(
        member * starts[None, :], axis=1
    )
    freqs = jnp.exp(jnp.arange(HEAD // 2, dtype=jnp.float32) * (-2.0 * math.log(10000.0) / HEAD))
    angles = places.astype(jnp.float32)[:, None] * freqs[None, :]
    return (jnp.cos(angles), jnp.sin(angles))


def masked_scores(queries, keys, mask):
    scores = jnp.einsum(
        "qhd,khd->hqk", queries, keys, preferred_element_type=jnp.float32
    ) * HEAD ** (-0.5)
    return jnp.where(mask[None], scores, -1e30)


def attend_forward(queries, keys, values, mask):
    scores = masked_scores(queries, keys, mask)
    top = jnp.max(scores, axis=-1, keepdims=True)
    expo = jnp.exp(scores - top)
    total = jnp.sum(expo, axis=-1, keepdims=True)
    probs = (expo / total).astype(jnp.bfloat16)
    output = jnp.einsum("hqk,khd->qhd", probs, values, preferred_element_type=jnp.float32)
    return (output, top + jnp.log(total))


def attend_backward(queries, keys, values, mask, log_total, grad_out, head_scale):
    probs = jnp.exp(masked_scores(queries, keys, mask) - log_total)
    grad_probs = jnp.einsum("qhd,khd->hqk", grad_out, values, preferred_element_type=jnp.float32)
    grad_probs = grad_probs * head_scale[:, None, None]
    grad_values = (
        jnp.einsum(
            "hqk,qhd->khd", probs.astype(jnp.bfloat16), grad_out, preferred_element_type=jnp.float32
        )
        * head_scale[None, :, None]
    )
    delta = jnp.sum(grad_probs * probs, axis=-1, keepdims=True)
    grad_scores = (probs * (grad_probs - delta)).astype(jnp.bfloat16)
    grad_queries = jnp.einsum(
        "hqk,khd->qhd", grad_scores, keys, preferred_element_type=jnp.float32
    ) * HEAD ** (-0.5)
    grad_keys = jnp.einsum(
        "hqk,qhd->khd", grad_scores, queries, preferred_element_type=jnp.float32
    ) * HEAD ** (-0.5)
    return (grad_queries, grad_keys, grad_values)


def narrow(values):
    return lax.optimization_barrier(values.astype(jnp.bfloat16)).astype(jnp.float32)


def shards(
    block_in,
    out_grad,
    condition,
    captions,
    caption_len,
    segment_ids,
    ada_weight,
    norm_gains,
    query_weight,
    key_weight,
    value_weight,
    head_gains,
    textkey_weight,
    textvalue_weight,
    cross_gate,
    out_weight,
    gate_weight,
    up_weight,
    down_weight,
):
    rows = block_in.shape[0]
    width = block_in.shape[1]
    length = segment_ids.shape[0]
    local_heads = cross_gate.shape[0]
    position = lax.axis_index("tensor")
    row_start = position * rows
    cond_act = jax.nn.silu(condition.astype(jnp.float32)).astype(jnp.bfloat16)
    ada_part = jnp.dot(cond_act, ada_weight, preferred_element_type=jnp.float32)
    modulation = lax.all_gather(ada_part, "tensor", axis=1, tiled=True)
    own_segments = lax.dynamic_slice_in_dim(segment_ids, row_start, rows)
    own_member = (own_segments[:, None] == jnp.arange(SEGS, dtype=jnp.int32)[None, :]).astype(
        jnp.float32
    )
    mod_rows = jnp.dot(own_member, modulation, precision=PRECISION)
    scale_attn = mod_rows[:, :width]
    gate_attn = mod_rows[:, width : 2 * width]
    scale_ffn = mod_rows[:, 2 * width : 3 * width]
    gate_ffn = mod_rows[:, 3 * width :]
    cosine, sine = rope_tables(segment_ids)
    self_mask = segment_ids[:, None] == segment_ids[None, :]
    key_segment = jnp.arange(SEGS * TXT, dtype=jnp.int32) // TXT
    key_place = jnp.arange(SEGS * TXT, dtype=jnp.int32) % TXT
    valid = key_place < caption_len[key_segment]
    cross_mask = (segment_ids[:, None] == key_segment[None, :]) & valid[None, :]
    block_f = block_in.astype(jnp.float32)
    attn_in_f, attn_in_pull = jax.vjp(norm_mod, block_f, norm_gains[0], scale_attn)
    attn_rows = lax.all_gather(attn_in_f.astype(jnp.bfloat16), "tensor", axis=0, tiled=True)
    raw_query = jnp.dot(attn_rows, query_weight, preferred_element_type=jnp.float32)
    raw_key = jnp.dot(attn_rows, key_weight, preferred_element_type=jnp.float32)
    values_b = jnp.dot(attn_rows, value_weight, preferred_element_type=jnp.float32).astype(
        jnp.bfloat16
    )
    values_b = values_b.reshape(length, local_heads, HEAD)

    def prepare(query_part, key_part, gain_query, gain_key):
        return (
            rotate(head_norm(query_part, gain_query), cosine, sine),
            rotate(head_norm(key_part, gain_key), cosine, sine),
        )

    (query_f, key_f), prep_pull = jax.vjp(prepare, raw_query, raw_key, head_gains[0], head_gains[1])
    queries_b = query_f.astype(jnp.bfloat16)
    keys_b = key_f.astype(jnp.bfloat16)
    caption_flat = captions.reshape(-1, captions.shape[-1])
    text_raw = jnp.dot(caption_flat, textkey_weight, preferred_element_type=jnp.float32)
    text_key_f, text_pull = jax.vjp(head_norm, text_raw, head_gains[2])
    text_keys_b = text_key_f.astype(jnp.bfloat16)
    text_values_b = jnp.dot(caption_flat, textvalue_weight, preferred_element_type=jnp.float32)
    text_values_b = text_values_b.astype(jnp.bfloat16).reshape(
        caption_flat.shape[0], local_heads, HEAD
    )
    self_out, self_log = attend_forward(queries_b, keys_b, values_b, self_mask)
    cross_out, cross_log = attend_forward(queries_b, text_keys_b, text_values_b, cross_mask)
    tanh_gate = jnp.tanh(cross_gate)
    mixed = (
        (self_out + tanh_gate[None, :, None] * cross_out).reshape(length, -1).astype(jnp.bfloat16)
    )
    attn_sum = lax.psum_scatter(
        jnp.dot(mixed, out_weight, preferred_element_type=jnp.float32).astype(jnp.bfloat16),
        "tensor",
        scatter_dimension=0,
        tiled=True,
    ).astype(jnp.float32)
    middle, mid_pull = jax.vjp(residual_add, block_f, attn_sum, norm_gains[1], gate_attn)
    ffn_in_f, ffn_in_pull = jax.vjp(norm_mod, middle, norm_gains[2], scale_ffn)
    ffn_rows = lax.all_gather(ffn_in_f.astype(jnp.bfloat16), "tensor", axis=0, tiled=True)
    gate_pre = jnp.dot(ffn_rows, gate_weight, preferred_element_type=jnp.float32)
    up_pre = jnp.dot(ffn_rows, up_weight, preferred_element_type=jnp.float32)
    sigmoid_gate = jax.nn.sigmoid(gate_pre)
    silu_gate = gate_pre * sigmoid_gate
    hidden = (silu_gate * up_pre).astype(jnp.bfloat16)
    ffn_sum = lax.psum_scatter(
        jnp.dot(hidden, down_weight, preferred_element_type=jnp.float32).astype(jnp.bfloat16),
        "tensor",
        scatter_dimension=0,
        tiled=True,
    ).astype(jnp.float32)
    block_out_f, post_pull = jax.vjp(residual_add, middle, ffn_sum, norm_gains[3], gate_ffn)
    grad_middle, grad_ffn, grad_gain_four, grad_gate_ffn = post_pull(out_grad.astype(jnp.float32))
    piece = lax.all_gather(grad_ffn.astype(jnp.bfloat16), "tensor", axis=0, tiled=True)
    part = times_transpose(piece, down_weight)
    grad_hidden = part
    used = hidden
    grad_hidden, down_grad = (grad_hidden, contract_rows(used, piece))
    grad_gate_b = (
        grad_hidden * up_pre * sigmoid_gate * (1.0 + gate_pre * (1.0 - sigmoid_gate))
    ).astype(jnp.bfloat16)
    grad_up_b = (grad_hidden * silu_gate).astype(jnp.bfloat16)
    gate_grad = contract_rows(ffn_rows, grad_gate_b)
    up_grad = contract_rows(ffn_rows, grad_up_b)
    grad_ffn_in = lax.psum_scatter(
        (times_transpose(grad_gate_b, gate_weight) + times_transpose(grad_up_b, up_weight)).astype(
            jnp.bfloat16
        ),
        "tensor",
        scatter_dimension=0,
        tiled=True,
    ).astype(jnp.float32)
    grad_mid_more, grad_gain_three, grad_scale_ffn = ffn_in_pull(grad_ffn_in)
    grad_middle = grad_middle + grad_mid_more
    grad_block, grad_attn, grad_gain_two, grad_gate_attn = mid_pull(grad_middle)
    piece = lax.all_gather(grad_attn.astype(jnp.bfloat16), "tensor", axis=0, tiled=True)
    part = times_transpose(piece, out_weight)
    grad_mixed = part
    used = mixed
    grad_mixed, outw_local = (grad_mixed, contract_rows(used, piece))
    grad_mixed_b = grad_mixed.astype(jnp.bfloat16).reshape(length, local_heads, HEAD)
    gate_term = jnp.sum(grad_mixed_b.astype(jnp.float32) * cross_out, axis=(0, 2)) * (
        1.0 - tanh_gate * tanh_gate
    )
    unit_scale = jnp.ones((local_heads,), jnp.float32)
    query_self, key_self, value_self = attend_backward(
        queries_b, keys_b, values_b, self_mask, self_log, grad_mixed_b, unit_scale
    )
    query_cross, text_key_back, text_value_back = attend_backward(
        queries_b, text_keys_b, text_values_b, cross_mask, cross_log, grad_mixed_b, tanh_gate
    )
    grad_raw_query, grad_raw_key, grad_gain_query, grad_gain_key = prep_pull(
        (narrow(query_self + query_cross), narrow(key_self))
    )
    grad_text_raw, grad_gain_text = text_pull(narrow(text_key_back))
    grad_query_b = grad_raw_query.astype(jnp.bfloat16)
    grad_key_b = grad_raw_key.astype(jnp.bfloat16)
    grad_value_b = value_self.reshape(length, -1).astype(jnp.bfloat16)
    query_grad = contract_rows(attn_rows, grad_query_b)
    key_grad = contract_rows(attn_rows, grad_key_b)
    value_grad = contract_rows(attn_rows, grad_value_b)
    textkey_grad = contract_rows(caption_flat, grad_text_raw.astype(jnp.bfloat16))
    textvalue_grad = contract_rows(
        caption_flat, text_value_back.reshape(caption_flat.shape[0], -1).astype(jnp.bfloat16)
    )
    query_part = grad_query_b
    key_part = grad_key_b
    grad_attn_in = lax.psum_scatter(
        (
            times_transpose(query_part, query_weight)
            + times_transpose(key_part, key_weight)
            + times_transpose(grad_value_b, value_weight)
        ).astype(jnp.bfloat16),
        "tensor",
        scatter_dimension=0,
        tiled=True,
    ).astype(jnp.float32)
    grad_block_more, grad_gain_one, grad_scale_attn = attn_in_pull(grad_attn_in)
    in_grad = (grad_block + grad_block_more).astype(jnp.bfloat16)
    grad_mod_rows = jnp.concatenate(
        [grad_scale_attn, grad_gate_attn, grad_scale_ffn, grad_gate_ffn], axis=1
    )
    grad_mod_part = lax.dot_general(
        own_member, grad_mod_rows, (((0,), (0,)), ((), ())), precision=PRECISION
    )
    grad_mod = lax.psum_scatter(
        grad_mod_part.astype(jnp.bfloat16), "tensor", scatter_dimension=1, tiled=True
    ).astype(jnp.float32)
    cond_wide = cond_act.astype(jnp.float32)
    ada_local = lax.dot_general(cond_wide, grad_mod, (((0,), (0,)), ((), ())), precision=PRECISION)
    ada_grad, query_sum, key_sum, value_sum, textkey_sum, textvalue_sum, gate_sum, up_sum = (
        lax.psum_scatter(
            ada_local.astype(jnp.bfloat16), "dp", scatter_dimension=0, tiled=True
        ).astype(jnp.float32),
        lax.psum_scatter(
            query_grad.astype(jnp.bfloat16), "dp", scatter_dimension=0, tiled=True
        ).astype(jnp.float32),
        lax.psum_scatter(
            key_grad.astype(jnp.bfloat16), "dp", scatter_dimension=0, tiled=True
        ).astype(jnp.float32),
        lax.psum_scatter(
            value_grad.astype(jnp.bfloat16), "dp", scatter_dimension=0, tiled=True
        ).astype(jnp.float32),
        lax.psum_scatter(
            textkey_grad.astype(jnp.bfloat16), "dp", scatter_dimension=0, tiled=True
        ).astype(jnp.float32),
        lax.psum_scatter(
            textvalue_grad.astype(jnp.bfloat16), "dp", scatter_dimension=0, tiled=True
        ).astype(jnp.float32),
        lax.psum_scatter(
            gate_grad.astype(jnp.bfloat16), "dp", scatter_dimension=0, tiled=True
        ).astype(jnp.float32),
        lax.psum_scatter(
            up_grad.astype(jnp.bfloat16), "dp", scatter_dimension=0, tiled=True
        ).astype(jnp.float32),
    )
    outw_sum, down_sum = (
        lax.psum_scatter(
            outw_local.astype(jnp.bfloat16), "dp", scatter_dimension=1, tiled=True
        ).astype(jnp.float32),
        lax.psum_scatter(
            down_grad.astype(jnp.bfloat16), "dp", scatter_dimension=1, tiled=True
        ).astype(jnp.float32),
    )
    gate_full = lax.dynamic_update_slice_in_dim(
        jnp.zeros((HEADS,), jnp.float32), gate_term, position * local_heads, 0
    )
    norm_stack = jnp.stack([grad_gain_one, grad_gain_two, grad_gain_three, grad_gain_four])
    head_stack = jnp.stack([grad_gain_query, grad_gain_key, grad_gain_text])
    norm_grads, head_grads, crossgate_grad = lax.psum(
        (norm_stack, head_stack, gate_full), ("dp", "tensor")
    )
    return (
        block_out_f.astype(jnp.bfloat16),
        in_grad,
        ada_grad,
        norm_grads,
        query_sum,
        key_sum,
        value_sum,
        head_grads,
        textkey_sum,
        textvalue_sum,
        crossgate_grad,
        outw_sum,
        gate_sum,
        up_sum,
        down_sum,
    )


def solution(mesh):
    return jax.shard_map(
        shards,
        mesh=mesh,
        in_specs=(
            P(("dp", "tensor"), None),
            P(("dp", "tensor"), None),
            P("dp", None),
            P("dp", None, None),
            P("dp"),
            P("dp"),
            P(None, "tensor"),
            P(),
            P(None, "tensor"),
            P(None, "tensor"),
            P(None, "tensor"),
            P(),
            P(None, "tensor"),
            P(None, "tensor"),
            P("tensor"),
            P("tensor", None),
            P(None, "tensor"),
            P(None, "tensor"),
            P("tensor", None),
        ),
        out_specs=(
            P(("dp", "tensor"), None),
            P(("dp", "tensor"), None),
            P("dp", "tensor"),
            P(),
            P("dp", "tensor"),
            P("dp", "tensor"),
            P("dp", "tensor"),
            P(),
            P("dp", "tensor"),
            P("dp", "tensor"),
            P(),
            P("tensor", "dp"),
            P("dp", "tensor"),
            P("dp", "tensor"),
            P("tensor", "dp"),
        ),
        check_vma=False,
    )
```

profile of v0, /device:TPU:0, one launch (start us, length us, event | category | flops | bytes accessed | tf_op | source)
XLA Modules:
  0.0 2657.2 jit_solution(10482225039872330956)
XLA Ops:
  13.1 5.8 all_gather.15
  31.7 5.1 copy.56
  36.9 7.6 multiply_reduce_fusion.2
  48.7 6.3 convolution_convert_fusion.13
  70.6 3.9 fusion.34
  79.7 26.6 %reduce-scatter.22.cloned.1.call-done = bf16[128,1536]{1,0:T(8,128)(2,1)} async-done(((bf16[512,1536]{1,0:T(8,128)(2,1)}), bf16[128,1536]{1,0:T(8,128)(2,1)}) %reduce-scatter.22.cloned.1.call-update) | async-done | bytes 393232 | tf_op jit(solution)/shard_map/reduce_scatter | solution.py:189
  112.9 25.9 all-gather.7.cloned.1.call-done
  138.7 4.3 fusion.109
  150.2 25.1 reduce-scatter.24.cloned.1.call-done
  182.4 25.7 all-gather.9.cloned.1.call-done
  208.1 5.2 multiply_convert_fusion.2
  219.0 25.1 reduce-scatter.26.cloned.1.call-done
  255.3 23.8 all-gather.11.cloned.1.call-done
  281.6 4.0 fusion.40
  285.7 7.5 multiply_reduce_fusion.1
  293.2 4.8 multiply_convert_fusion.1
  317.1 25.1 reduce-scatter.28.cloned.1.call-done
  373.4 4.9 fusion.30
  378.3 5.6 fusion.4
  392.4 5.6 fusion.3
  401.6 3.8 convolution_convert_fusion.6
  411.8 193.9 %reduce-scatter.44.cloned.1.call-done = bf16[1024,48]{0,1:T(8,128)(2,1)} async-done(((bf16[1024,1536]{0,1:T(8,128)(2,1)}), bf16[1024,48]{0,1:T(8,128)(2,1)}) %reduce-scatter.44.cloned.1.call-update) | async-done | bytes 98320 | tf_op jit(solution)/shard_map/reduce_scatter | solution.py:318
  607.3 227.1 %reduce-scatter.42.cloned.1.call-done = bf16[48,1024]{1,0:T(8,128)(2,1)} async-done(((bf16[1536,1024]{1,0:T(8,128)(2,1)}), bf16[48,1024]{1,0:T(8,128)(2,1)}) %reduce-scatter.42.cloned.1.call-update) | async-done | bytes 98320 | tf_op jit(solution)/shard_map/reduce_scatter | solution.py:310
  836.0 226.2 %reduce-scatter.40.cloned.1.call-done = bf16[48,1024]{1,0:T(8,128)(2,1)} async-done(((bf16[1536,1024]{1,0:T(8,128)(2,1)}), bf16[48,1024]{1,0:T(8,128)(2,1)}) %reduce-scatter.40.cloned.1.call-update) | async-done | bytes 98320 | tf_op jit(solution)/shard_map/reduce_scatter | solution.py:307
  1063.8 223.9 %reduce-scatter.38.cloned.1.call-done = bf16[384,48]{0,1:T(8,128)(2,1)} async-done(((bf16[384,1536]{0,1:T(8,128)(2,1)}), bf16[384,48]{0,1:T(8,128)(2,1)}) %reduce-scatter.38.cloned.1.call-update) | async-done | bytes 36880 | tf_op jit(solution)/shard_map/reduce_scatter | solution.py:315
  1289.1 223.9 %reduce-scatter.36.cloned.1.call-done = bf16[48,384]{1,0:T(8,128)(2,1)} async-done(((bf16[1536,384]{1,0:T(8,128)(2,1)}), bf16[48,384]{1,0:T(8,128)(2,1)}) %reduce-scatter.36.cloned.1.call-update) | async-done | bytes 36880 | tf_op jit(solution)/shard_map/reduce_scatter | solution.py:298
  1514.4 223.8 %reduce-scatter.34.cloned.1.call-done = bf16[48,384]{1,0:T(8,128)(2,1)} async-done(((bf16[1536,384]{1,0:T(8,128)(2,1)}), bf16[48,384]{1,0:T(8,128)(2,1)}) %reduce-scatter.34.cloned.1.call-update) | async-done | bytes 36880 | tf_op jit(solution)/shard_map/reduce_scatter | solution.py:295
  1739.6 223.8 %reduce-scatter.32.cloned.1.call-done = bf16[48,384]{1,0:T(8,128)(2,1)} async-done(((bf16[1536,384]{1,0:T(8,128)(2,1)}), bf16[48,384]{1,0:T(8,128)(2,1)}) %reduce-scatter.32.cloned.1.call-update) | async-done | bytes 36880 | tf_op jit(solution)/shard_map/reduce_scatter | solution.py:292
  1966.2 63.9 %all-reduce.4 = (f32[4,1536]{1,0:T(4,128)}, f32[3,64]{1,0:T(4,128)}, f32[24]{0:T(128)}) all-reduce(f32[4,1536]{1,0:T(4,128)} %pad_maximum_fusion.4, f32[3,64]{1,0:T(4,128)} %pad_maximum_fusion.5, f32[24]{0:T(128)} %multiply_dynamic-update-slice_fusion), channel_id=1, replica_groups=mesh['dp'=32,'tensor'=4] {'dp','tensor'}, use_global_device_ids=true, to_apply=%region_31.32 | all-reduce | flops 6360 | bytes 50880 | tf_op jit(solution)/shard_map/psum | solution.py:327
  2033.2 159.0 %reduce-scatter.50.cloned.1.call-done = bf16[128,384]{1,0:T(8,128)(2,1)} async-done(((bf16[4096,384]{1,0:T(8,128)(2,1)}), bf16[128,384]{1,0:T(8,128)(2,1)}) %reduce-scatter.50.cloned.1.call-update) | async-done | bytes 98320
  2194.1 226.1 %reduce-scatter.48.cloned.1.call-done = bf16[128,384]{1,0:T(8,128)(2,1)} async-done(((bf16[4096,384]{1,0:T(8,128)(2,1)}), bf16[128,384]{1,0:T(8,128)(2,1)}) %reduce-scatter.48.cloned.1.call-update) | async-done | bytes 98320
  2421.9 227.0 %reduce-scatter.30.cloned.1.call-done = bf16[32,1536]{1,0:T(8,128)(2,1)} async-done(((bf16[1024,1536]{1,0:T(8,128)(2,1)}), bf16[32,1536]{1,0:T(8,128)(2,1)}) %reduce-scatter.30.cloned.1.call-update) | async-done | bytes 98320 | tf_op jit(solution)/shard_map/reduce_scatter | solution.py:289
  (411 shorter events, 171.4 us)
Async XLA Ops:
  7.2 140.0 %copy-start = (bf16[1024,1536]{1,0:T(8,128)(2,1)S(1)}, bf16[1024,1536]{1,0:T(8,128)(2,1)}, u32[]{:S(2)}) copy-start(bf16[1024,1536]{1,0:T(8,128)(2,1)} %param.37) | copy-start | bytes 9437188
  7.2 47.7 %all-gather.5.cloned.1.call-start = ((), (), s32[]{:S(2)}) async-start(), calls=%async_computation.15 | async-start | bytes 1966080 | tf_op jit(solution)/shard_map/all_gather | solution.py:158
  10.6 12.9 copy-start.18
  24.5 81.8 %reduce-scatter.22.cloned.1.call-start = ((), (), s32[]{:S(2)}) async-start(), calls=%async_computation.16 | async-start | bytes 1966080 | tf_op jit(solution)/shard_map/reduce_scatter | solution.py:189
  61.8 13.5 copy-start.3
  61.8 13.5 copy-start.76
  79.6 59.1 %all-gather.7.cloned.1.call-start = ((), (), s32[]{:S(2)}) async-start(), calls=%async_computation.17 | async-start | bytes 1966080 | tf_op jit(solution)/shard_map/all_gather | solution.py:197
  112.8 62.5 %reduce-scatter.24.cloned.1.call-start = ((), (), s32[]{:S(2)}) async-start(), calls=%async_computation.18 | async-start | bytes 1966080 | tf_op jit(solution)/shard_map/reduce_scatter | solution.py:203
  147.2 29.3 %copy-start.22 = (bf16[128,1536]{1,0:T(8,128)(2,1)S(1)}, bf16[128,1536]{1,0:T(8,128)(2,1)}, u32[]{:S(2)}) copy-start(bf16[128,1536]{1,0:T(8,128)(2,1)} %param.20) | copy-start | bytes 1179652
  150.2 57.9 %all-gather.9.cloned.1.call-start = ((), (), s32[]{:S(2)}) async-start(), calls=%async_computation.19 | async-start | bytes 1966080 | tf_op jit(solution)/shard_map/all_gather | solution.py:211
  182.2 62.0 %reduce-scatter.26.cloned.1.call-start = ((), (), s32[]{:S(2)}) async-start(), calls=%async_computation.20 | async-start | bytes 1966080 | tf_op jit(solution)/shard_map/reduce_scatter | solution.py:222
  215.9 28.2 %copy-start.6 = (f32[128,6144]{1,0:T(8,128)S(1)}, f32[128,6144]{1,0:T(8,128)}, u32[]{:S(2)}) copy-start(f32[128,6144]{1,0:T(8,128)} %copy-done.5) | copy-start | bytes 9437188
  219.0 29.1 %copy-start.17 = (bf16[128,1536]{1,0:T(8,128)(2,1)S(1)}, bf16[128,1536]{1,0:T(8,128)(2,1)}, u32[]{:S(2)}) copy-start(bf16[128,1536]{1,0:T(8,128)(2,1)} %reduce-scatter.22.cloned.1.call-done) | copy-start | bytes 1179652
  219.0 60.0 %all-gather.11.cloned.1.call-start = ((), (), s32[]{:S(2)}) async-start(), calls=%async_computation.21 | async-start | bytes 1966080 | tf_op jit(solution)/shard_map/all_gather | solution.py:233
  253.1 89.1 %reduce-scatter.28.cloned.1.call-start = ((), (), s32[]{:S(2)}) async-start(), calls=%async_computation.22 | async-start | bytes 1966080 | tf_op jit(solution)/shard_map/reduce_scatter | solution.py:265
  253.9 31.8 %copy-start.65 = (f32[6,512]{1,0:T(8,128)}, f32[6,512]{1,0:T(8,128)S(1)}, u32[]{:S(2)}) copy-start(f32[6,512]{1,0:T(8,128)S(1)} %log_add_fusion.1) | copy-start | bytes 36868
  281.6 18.3 copy-start.20
  285.7 28.9 %copy-start.30 = (bf16[6,64,512]{2,1,0:T(8,128)(2,1)}, bf16[6,64,512]{2,1,0:T(8,128)(2,1)S(1)}, u32[]{:S(2)}) copy-start(bf16[6,64,512]{2,1,0:T(8,128)(2,1)S(1)} %fusion.40) | copy-start | bytes 1179652
  314.8 27.4 %copy-start.19 = (bf16[128,1536]{1,0:T(8,128)(2,1)S(1)}, bf16[128,1536]{1,0:T(8,128)(2,1)}, u32[]{:S(2)}) copy-start(bf16[128,1536]{1,0:T(8,128)(2,1)} %param.19) | copy-start | bytes 1179652
  314.8 27.4 %copy-start.73 = (f32[1536]{0:T(1024)S(1)}, f32[1536]{0:T(1024)}, u32[]{:S(2)}) copy-start(f32[1536]{0:T(1024)} %copy-done.72) | copy-start | bytes 18436
  317.1 83.9 %reduce-scatter.46.cloned.1.call-start = ((), (), s32[]{:S(2)}) async-start(), calls=%async_computation.31 | async-start | bytes 1966080
  348.9 256.8 %reduce-scatter.44.cloned.1.call-start = ((), (), s32[]{:S(2)}) async-start(), calls=%async_computation.30 | async-start | bytes 3244032 | tf_op jit(solution)/shard_map/reduce_scatter | solution.py:318
  352.5 482.0 %reduce-scatter.42.cloned.1.call-start = ((), (), s32[]{:S(2)}) async-start(), calls=%async_computation.29 | async-start | bytes 3244032 | tf_op jit(solution)/shard_map/reduce_scatter | solution.py:310
  357.6 704.6 %reduce-scatter.40.cloned.1.call-start = ((), (), s32[]{:S(2)}) async-start(), calls=%async_computation.28 | async-start | bytes 3244032 | tf_op jit(solution)/shard_map/reduce_scatter | solution.py:307
  362.4 925.3 %reduce-scatter.38.cloned.1.call-start = ((), (), s32[]{:S(2)}) async-start(), calls=%async_computation.27 | async-start | bytes 1216512 | tf_op jit(solution)/shard_map/reduce_scatter | solution.py:315
  366.9 1146.1 %reduce-scatter.36.cloned.1.call-start = ((), (), s32[]{:S(2)}) async-start(), calls=%async_computation.26 | async-start | bytes 1216512 | tf_op jit(solution)/shard_map/reduce_scatter | solution.py:298
  369.1 1369.1 %reduce-scatter.34.cloned.1.call-start = ((), (), s32[]{:S(2)}) async-start(), calls=%async_computation.25 | async-start | bytes 1216512 | tf_op jit(solution)/shard_map/reduce_scatter | solution.py:295
  371.2 1592.2 %reduce-scatter.32.cloned.1.call-start = ((), (), s32[]{:S(2)}) async-start(), calls=%async_computation.24 | async-start | bytes 1216512 | tf_op jit(solution)/shard_map/reduce_scatter | solution.py:292
  373.4 1818.9 %reduce-scatter.50.cloned.1.call-start = ((), (), s32[]{:S(2)}) async-start(), calls=%async_computation.33 | async-start | bytes 3244032
  386.9 2033.3 %reduce-scatter.48.cloned.1.call-start = ((), (), s32[]{:S(2)}) async-start(), calls=%async_computation.32 | async-start | bytes 3244032
  400.9 2248.0 %reduce-scatter.30.cloned.1.call-start = ((), (), s32[]{:S(2)}) async-start(), calls=%async_computation.23 | async-start | bytes 3244032 | tf_op jit(solution)/shard_map/reduce_scatter | solution.py:289
  407.2 2243.3 %copy-start.1 = (bf16[1024,1536]{1,0:T(8,128)(2,1)S(1)}, bf16[1024,1536]{1,0:T(8,128)(2,1)}, u32[]{:S(2)}) copy-start(bf16[1024,1536]{1,0:T(8,128)(2,1)} %param.37) | copy-start | bytes 9437188
  (114 other events, 360.2 us)
Sparse Core Ops, SparseCore 0:
  24.6 27.2 all-gather.4
  79.7 26.4 reduce-scatter.21
  112.9 25.7 all-gather.6
  150.3 24.9 reduce-scatter.23
  182.3 25.7 all-gather.8
  219.1 24.9 reduce-scatter.25
  253.2 25.7 all-gather.10
  317.2 24.9 reduce-scatter.27
  349.0 24.9 reduce-scatter.45
  378.8 226.8 reduce-scatter.43
  611.4 222.9 reduce-scatter.41
  839.2 222.9 reduce-scatter.39
  1067.8 219.8 reduce-scatter.37
  1293.1 219.7 reduce-scatter.35
  1518.4 219.7 reduce-scatter.33
  1743.7 219.7 reduce-scatter.31
  1969.0 223.2 reduce-scatter.49
  2197.1 223.0 reduce-scatter.47
  2425.9 223.0 reduce-scatter.29
where the time goes:
time: 2660 us
  waiting for transfers between devices  2330 us (88%)
  matrix products  126 us (5%)
  blocking collectives  69.7 us (3%)
  other arithmetic  68.6 us (3%)
  local copies, waits for them, and re-layouts  43.4 us (2%)
    unnamed x22, waiting for transfers between devices  385 us
    reduce_scatter x1, waiting for transfers between devices, shards(): lax.psum_scatter(up_grad.astype(jnp.bfloat16), 'dp', scatter_dimension=0,...  227 us
    reduce_scatter x1, waiting for transfers between devices, shards(): lax.psum_scatter(ada_local.astype(jnp.bfloat16), 'dp', scatter_dimension=...  227 us
    reduce_scatter x1, waiting for transfers between devices, shards(): lax.psum_scatter(gate_grad.astype(jnp.bfloat16), 'dp', scatter_dimension=...  226 us
    reduce_scatter x1, waiting for transfers between devices, shards(): lax.psum_scatter(value_grad.astype(jnp.bfloat16), 'dp', scatter_dimension...  224 us
    reduce_scatter x1, waiting for transfers between devices, shards(): lax.psum_scatter(outw_local.astype(jnp.bfloat16), 'dp', scatter_dimension...  224 us
    reduce_scatter x1, waiting for transfers between devices, shards(): lax.psum_scatter(key_grad.astype(jnp.bfloat16), 'dp', scatter_dimension=0...  224 us
    reduce_scatter x1, waiting for transfers between devices, shards(): lax.psum_scatter(query_grad.astype(jnp.bfloat16), 'dp', scatter_dimension...  224 us
  transfers between devices with their start and end apart: 19, of which 17 were waited for; matrix products, arithmetic and copies ran while one was open for 4% of the time, Pallas kernels for 0%

commit v1 on v0

v1 whole, which is shorter than its diff:
```python
import math

import jax
import jax.numpy as jnp
from jax import lax
from jax.sharding import PartitionSpec as P

HEAD = 64
HEADS = 24
TXT = 256
SEGS = 3
EPS = 1e-06
PRECISION = lax.Precision.HIGHEST

RING = 4
PAIR = 2
CORE_SWAP = [(0, 1), (1, 0), (2, 3), (3, 2)]
CHIP_SWAP = [(0, 2), (2, 0), (1, 3), (3, 1)]


def dp_index(x, z, y):
    return (x * PAIR + z) * RING + y


def dp_perm(axis, step):
    pairs = []
    for x in range(RING):
        for z in range(PAIR):
            for y in range(RING):
                target = {
                    "x": ((x + step) % RING, z, y),
                    "y": (x, z, (y + step) % RING),
                    "z": (x, (z + step) % PAIR, y),
                }[axis]
                pairs.append((dp_index(x, z, y), dp_index(*target)))
    return pairs


def dp_place():
    index = lax.axis_index("dp")
    return {"x": index // (RING * PAIR), "z": index // RING % PAIR, "y": index % RING}


def swap_core(values):
    return lax.ppermute(values, "tensor", CORE_SWAP)


def swap_chip(values):
    return lax.ppermute(values, "tensor", CHIP_SWAP)


def contract_rows(left, right):
    return lax.dot_general(
        left, right, (((0,), (0,)), ((), ())), preferred_element_type=jnp.float32
    )


def times_transpose(left, right):
    return lax.dot_general(
        left, right, (((1,), (1,)), ((), ())), preferred_element_type=jnp.float32
    )


def gather_tensor(block):
    far = swap_chip(block)
    near = swap_core(block)
    return [block, near, far, swap_core(far)]


def scatter_tensor(blocks):
    near = swap_core(jnp.concatenate([blocks[1], blocks[3]], axis=0))
    rows = blocks[0].shape[0]
    far = (blocks[2].astype(jnp.float32) + near[rows:].astype(jnp.float32)).astype(near.dtype)
    return (
        blocks[0].astype(jnp.float32)
        + near[:rows].astype(jnp.float32)
        + swap_chip(far).astype(jnp.float32)
    )


def pick(stacked, index):
    return lax.dynamic_index_in_dim(stacked, index, 0, keepdims=False)


def gather_dp(block):
    block = block[None]
    for axis, size in (("z", PAIR), ("y", RING), ("x", RING)):
        block = jnp.concatenate(
            [block] + [lax.ppermute(block, "dp", dp_perm(axis, step)) for step in range(1, size)],
            axis=0,
        )
    return block


def scatter_stage(chunk_of, axis, place, size):
    total = chunk_of(place).astype(jnp.float32)
    for step in range(1, size):
        sent = chunk_of((place + step) % size)
        total = total + lax.ppermute(sent, "dp", dp_perm(axis, step)).astype(jnp.float32)
    return total


def scatter_dp(first_parts, second_parts, place):
    def whole(parts):
        return [
            part.reshape(RING, PAIR, RING, part.shape[0] // (RING * PAIR * RING), part.shape[1])
            for part in parts
        ]

    def along(parts, axis):
        def chunk_of(index):
            return jnp.concatenate(
                [
                    lax.dynamic_index_in_dim(part, index, axis, keepdims=False)
                    for part in parts
                ],
                axis=-1,
            )

        return chunk_of

    by_x = scatter_stage(along(whole(first_parts), 0), "x", place["x"], RING)
    by_y = scatter_stage(along(whole(second_parts), 2), "y", place["y"], RING)
    by_x = by_x.astype(jnp.bfloat16)
    by_y = by_y.astype(jnp.bfloat16)
    by_x = scatter_stage(along([by_x], 1), "y", place["y"], RING)
    by_y = scatter_stage(along([by_y], 0), "x", place["x"], RING)
    both = jnp.concatenate([by_x, by_y], axis=-1).astype(jnp.bfloat16)
    return scatter_stage(along([both], 0), "z", place["z"], PAIR)


def inverse_rms(values):
    return lax.rsqrt(jnp.mean(values * values, axis=-1, keepdims=True) + EPS)


def head_norm(values, gain):
    values = values.reshape(values.shape[0], -1, HEAD)
    return values * inverse_rms(values) * gain


def rotate(values, cosine, sine):
    half = HEAD // 2
    first = values[..., :half]
    second = values[..., half:]
    cosine = cosine[:, None, :]
    sine = sine[:, None, :]
    return jnp.concatenate(
        [first * cosine - second * sine, first * sine + second * cosine], axis=-1
    )


def rope_tables(segments, tokens, whole_segments):
    labels = jnp.arange(SEGS, dtype=jnp.int32)
    starts = jnp.sum((whole_segments[None, :] < labels[:, None]).astype(jnp.int32), axis=1)
    member = (segments[:, None] == labels[None, :]).astype(jnp.int32)
    places = tokens - jnp.sum(member * starts[None, :], axis=1)
    freqs = jnp.exp(jnp.arange(HEAD // 2, dtype=jnp.float32) * (-2.0 * math.log(10000.0) / HEAD))
    angles = places.astype(jnp.float32)[:, None] * freqs[None, :]
    return (jnp.cos(angles), jnp.sin(angles))


def masked_scores(queries, keys, mask):
    scores = jnp.einsum(
        "qhd,khd->hqk", queries, keys, preferred_element_type=jnp.float32
    ) * HEAD ** (-0.5)
    return jnp.where(mask[None], scores, -1e30)


def attend_forward(queries, keys, values, mask):
    scores = masked_scores(queries, keys, mask)
    top = jnp.max(scores, axis=-1, keepdims=True)
    expo = jnp.exp(scores - top)
    total = jnp.sum(expo, axis=-1, keepdims=True)
    probs = (expo / total).astype(jnp.bfloat16)
    output = jnp.einsum("hqk,khd->qhd", probs, values, preferred_element_type=jnp.float32)
    return (output, top + jnp.log(total))


def attend_backward(queries, keys, values, mask, log_total, grad_out, head_scale):
    probs = jnp.exp(masked_scores(queries, keys, mask) - log_total)
    grad_probs = jnp.einsum("qhd,khd->hqk", grad_out, values, preferred_element_type=jnp.float32)
    grad_probs = grad_probs * head_scale[:, None, None]
    grad_values = (
        jnp.einsum(
            "hqk,qhd->khd", probs.astype(jnp.bfloat16), grad_out, preferred_element_type=jnp.float32
        )
        * head_scale[None, :, None]
    )
    delta = jnp.sum(grad_probs * probs, axis=-1, keepdims=True)
    grad_scores = (probs * (grad_probs - delta)).astype(jnp.bfloat16)
    grad_queries = jnp.einsum(
        "hqk,khd->qhd", grad_scores, keys, preferred_element_type=jnp.float32
    ) * HEAD ** (-0.5)
    grad_keys = jnp.einsum(
        "hqk,qhd->khd", grad_scores, queries, preferred_element_type=jnp.float32
    ) * HEAD ** (-0.5)
    return (grad_queries, grad_keys, grad_values)


def narrow(values):
    return lax.optimization_barrier(values.astype(jnp.bfloat16)).astype(jnp.float32)


def shards(
    block_in,
    out_grad,
    condition,
    captions,
    caption_len,
    segment_ids,
    ada_weight,
    norm_gains,
    query_weight,
    key_weight,
    value_weight,
    head_gains,
    textkey_weight,
    textvalue_weight,
    cross_gate,
    out_weight,
    gate_weight,
    up_weight,
    down_weight,
):
    rows, width = block_in.shape
    length = segment_ids.shape[0]
    parts = length // rows
    local_heads = cross_gate.shape[0]
    position = lax.axis_index("tensor")
    place = dp_place()

    all_rows = jnp.concatenate(gather_tensor(block_in), axis=0)
    own_act = jax.nn.silu(condition.astype(jnp.float32)).astype(jnp.bfloat16)
    own_part = jnp.dot(own_act, ada_weight, preferred_element_type=jnp.float32)
    near_first = jnp.stack(gather_tensor(own_part))
    scale_attn, gate_attn, scale_ffn, gate_ffn = [
        pick(near_first, jnp.bitwise_xor(position, block)) for block in range(parts)
    ]
    order = [jnp.bitwise_xor(position, block) for block in range(parts)]
    segments = jnp.concatenate(
        [lax.dynamic_slice_in_dim(segment_ids, block * rows, rows) for block in order]
    )
    tokens = jnp.concatenate([block * rows + jnp.arange(rows, dtype=jnp.int32) for block in order])
    own_segments = segments[:rows]
    own_member = (own_segments[:, None] == jnp.arange(SEGS, dtype=jnp.int32)[None, :]).astype(
        jnp.float32
    )

    def per_row(table, ids):
        ids = ids[:, None]
        return jnp.where(ids == 0, table[0], jnp.where(ids == 1, table[1], table[2]))

    def segment_sum(values):
        return lax.dot_general(
            own_member, values, (((0,), (0,)), ((), ())), precision=PRECISION
        )

    cosine, sine = rope_tables(segments, tokens, segment_ids)
    self_mask = segments[:, None] == segments[None, :]
    key_segment = jnp.arange(SEGS * TXT, dtype=jnp.int32) // TXT
    key_place = jnp.arange(SEGS * TXT, dtype=jnp.int32) % TXT
    valid = key_place < jnp.repeat(caption_len, TXT)
    cross_mask = (segments[:, None] == key_segment[None, :]) & valid[None, :]

    all_f = all_rows.astype(jnp.float32)
    attn_rows = (
        all_f * inverse_rms(all_f) * norm_gains[0] * (1.0 + per_row(scale_attn, segments))
    ).astype(jnp.bfloat16)
    raw_query = jnp.dot(attn_rows, query_weight, preferred_element_type=jnp.float32)
    raw_key = jnp.dot(attn_rows, key_weight, preferred_element_type=jnp.float32)
    values_b = jnp.dot(attn_rows, value_weight, preferred_element_type=jnp.float32).astype(
        jnp.bfloat16
    )
    values_b = values_b.reshape(length, local_heads, HEAD)

    def prepare(query_part, key_part, gain_query, gain_key):
        return (
            rotate(head_norm(query_part, gain_query), cosine, sine),
            rotate(head_norm(key_part, gain_key), cosine, sine),
        )

    (query_f, key_f), prep_pull = jax.vjp(prepare, raw_query, raw_key, head_gains[0], head_gains[1])
    queries_b = query_f.astype(jnp.bfloat16)
    keys_b = key_f.astype(jnp.bfloat16)
    caption_flat = captions.reshape(-1, captions.shape[-1])
    text_raw = jnp.dot(caption_flat, textkey_weight, preferred_element_type=jnp.float32)
    text_key_f, text_pull = jax.vjp(head_norm, text_raw, head_gains[2])
    text_keys_b = text_key_f.astype(jnp.bfloat16)
    text_values_b = jnp.dot(caption_flat, textvalue_weight, preferred_element_type=jnp.float32)
    text_values_b = text_values_b.astype(jnp.bfloat16).reshape(
        caption_flat.shape[0], local_heads, HEAD
    )
    self_out, self_log = attend_forward(queries_b, keys_b, values_b, self_mask)
    cross_out, cross_log = attend_forward(queries_b, text_keys_b, text_values_b, cross_mask)
    tanh_gate = jnp.tanh(cross_gate)
    mixed = (
        (self_out + tanh_gate[None, :, None] * cross_out).reshape(length, -1).astype(jnp.bfloat16)
    )

    def row_blocks(values):
        values = values.astype(jnp.bfloat16)
        return [values[block * rows : (block + 1) * rows] for block in range(parts)]

    def all_of(block):
        return jnp.concatenate(gather_tensor(block.astype(jnp.bfloat16)), axis=0)

    attn_sum = scatter_tensor(
        row_blocks(jnp.dot(mixed, out_weight, preferred_element_type=jnp.float32))
    )
    block_f = block_in.astype(jnp.float32)
    attn_inv = inverse_rms(attn_sum)
    attn_unit = attn_sum * attn_inv
    attn_factor = jnp.tanh(per_row(gate_attn, own_segments)) * norm_gains[1]
    middle = block_f + attn_factor * attn_unit
    mid_inv = inverse_rms(middle)
    mid_unit = middle * mid_inv
    mid_factor = norm_gains[2] * (1.0 + per_row(scale_ffn, own_segments))
    ffn_rows = all_of(mid_unit * mid_factor)
    gate_pre = jnp.dot(ffn_rows, gate_weight, preferred_element_type=jnp.float32)
    up_pre = jnp.dot(ffn_rows, up_weight, preferred_element_type=jnp.float32)
    sigmoid_gate = jax.nn.sigmoid(gate_pre)
    silu_gate = gate_pre * sigmoid_gate
    hidden = (silu_gate * up_pre).astype(jnp.bfloat16)
    ffn_sum = scatter_tensor(
        row_blocks(jnp.dot(hidden, down_weight, preferred_element_type=jnp.float32))
    )
    ffn_inv = inverse_rms(ffn_sum)
    ffn_unit = ffn_sum * ffn_inv
    ffn_factor = jnp.tanh(per_row(gate_ffn, own_segments)) * norm_gains[3]
    block_out = (middle + ffn_factor * ffn_unit).astype(jnp.bfloat16)

    def norm_back(weighted, unit, inverse):
        return inverse * (weighted - unit * jnp.mean(weighted * unit, axis=-1, keepdims=True))

    grad_out = out_grad.astype(jnp.float32)
    sum_gate_ffn = segment_sum(grad_out * ffn_unit)
    grad_ffn = all_of(norm_back(grad_out * ffn_factor, ffn_unit, ffn_inv))
    grad_hidden = times_transpose(grad_ffn, down_weight)
    down_grad = contract_rows(grad_ffn, hidden).astype(jnp.bfloat16)
    grad_gate_b = (
        grad_hidden * up_pre * sigmoid_gate * (1.0 + gate_pre * (1.0 - sigmoid_gate))
    ).astype(jnp.bfloat16)
    grad_up_b = (grad_hidden * silu_gate).astype(jnp.bfloat16)
    grad_ffn_in = scatter_tensor(
        row_blocks(
            times_transpose(grad_gate_b, gate_weight) + times_transpose(grad_up_b, up_weight)
        )
    )
    gate_grad = contract_rows(ffn_rows, grad_gate_b).astype(jnp.bfloat16)
    up_grad = contract_rows(ffn_rows, grad_up_b).astype(jnp.bfloat16)
    sum_scale_ffn = segment_sum(grad_ffn_in * mid_unit)
    grad_middle = grad_out + norm_back(grad_ffn_in * mid_factor, mid_unit, mid_inv)
    sum_gate_attn = segment_sum(grad_middle * attn_unit)
    grad_attn = all_of(norm_back(grad_middle * attn_factor, attn_unit, attn_inv))
    grad_mixed_b = times_transpose(grad_attn, out_weight).astype(jnp.bfloat16)
    outw_grad = contract_rows(grad_attn, mixed).astype(jnp.bfloat16)
    grad_mixed_b = grad_mixed_b.reshape(length, local_heads, HEAD)
    gate_term = jnp.sum(grad_mixed_b.astype(jnp.float32) * cross_out, axis=(0, 2)) * (
        1.0 - tanh_gate * tanh_gate
    )
    unit_scale = jnp.ones((local_heads,), jnp.float32)
    query_cross, text_key_back, text_value_back = attend_backward(
        queries_b, text_keys_b, text_values_b, cross_mask, cross_log, grad_mixed_b, tanh_gate
    )
    query_self, key_self, value_self = attend_backward(
        queries_b, keys_b, values_b, self_mask, self_log, grad_mixed_b, unit_scale
    )
    grad_text_raw, grad_gain_text = text_pull(narrow(text_key_back))
    textkey_grad = contract_rows(caption_flat, grad_text_raw.astype(jnp.bfloat16))
    textvalue_grad = contract_rows(
        caption_flat, text_value_back.reshape(caption_flat.shape[0], -1).astype(jnp.bfloat16)
    )
    grad_raw_query, grad_raw_key, grad_gain_query, grad_gain_key = prep_pull(
        (narrow(query_self + query_cross), narrow(key_self))
    )
    grad_query_b = grad_raw_query.astype(jnp.bfloat16)
    grad_key_b = grad_raw_key.astype(jnp.bfloat16)
    grad_value_b = value_self.reshape(length, -1).astype(jnp.bfloat16)
    grad_attn_in = scatter_tensor(
        row_blocks(
            times_transpose(grad_query_b, query_weight)
            + times_transpose(grad_key_b, key_weight)
            + times_transpose(grad_value_b, value_weight)
        )
    )
    query_grad = contract_rows(attn_rows, grad_query_b).astype(jnp.bfloat16)
    key_grad = contract_rows(attn_rows, grad_key_b).astype(jnp.bfloat16)
    value_grad = contract_rows(attn_rows, grad_value_b).astype(jnp.bfloat16)
    block_inv = inverse_rms(block_f)
    block_unit = block_f * block_inv
    block_factor = norm_gains[0] * (1.0 + per_row(scale_attn, own_segments))
    sum_scale_attn = segment_sum(grad_attn_in * block_unit)
    in_grad = (
        grad_middle + norm_back(grad_attn_in * block_factor, block_unit, block_inv)
    ).astype(jnp.bfloat16)

    half = down_grad.shape[1] // 2
    ffn_group = scatter_dp(
        [gate_grad, down_grad[:, :half]], [up_grad, down_grad[:, half:]], place
    )
    text_group = scatter_dp(
        [textkey_grad.astype(jnp.bfloat16)], [textvalue_grad.astype(jnp.bfloat16)], place
    )
    attn_group = scatter_dp([query_grad, key_grad], [value_grad, outw_grad], place)
    hidden_cols = gate_grad.shape[1]
    gate_sum = ffn_group[:, :hidden_cols]
    up_sum = ffn_group[:, hidden_cols + half : 2 * hidden_cols + half]
    down_sum = jnp.concatenate(
        [ffn_group[:, hidden_cols : hidden_cols + half], ffn_group[:, 2 * hidden_cols + half :]],
        axis=1,
    ).T
    head_cols = query_grad.shape[1]
    query_sum, key_sum, value_sum, outw_sum = [
        attn_group[:, block * head_cols : (block + 1) * head_cols] for block in range(4)
    ]
    textkey_sum = text_group[:, :head_cols]
    textvalue_sum = text_group[:, head_cols:]

    sums = jnp.stack([sum_scale_attn, sum_gate_attn, sum_scale_ffn, sum_gate_ffn])
    own_sum = scatter_tensor([pick(sums, block) for block in order])
    gate_full = lax.dynamic_update_slice_in_dim(
        jnp.zeros((HEADS,), jnp.float32), gate_term, position * local_heads, 0
    )
    extras = jnp.concatenate([grad_gain_query, grad_gain_key, grad_gain_text, gate_full])
    extras = jnp.pad(extras, (0, width - extras.shape[0]))
    gathered = gather_dp(jnp.concatenate([own_sum, extras[None]], axis=0))
    conditions = gather_dp(condition).reshape(-1, condition.shape[1])
    acts = jax.nn.silu(conditions.astype(jnp.float32)).astype(jnp.bfloat16)
    parts_all = jnp.dot(acts, ada_weight, preferred_element_type=jnp.float32)
    all_sums = gathered[:, :SEGS].reshape(-1, width)
    is_gate = position % 2 == 1
    tanh_all = jnp.tanh(parts_all)
    factor = jnp.where(is_gate, tanh_all, 1.0 + parts_all)
    slope = jnp.where(is_gate, 1.0 - tanh_all * tanh_all, 1.0)
    grad_mod = all_sums * slope * pick(norm_gains, position)
    ada_rows = acts.shape[1] // (RING * PAIR * RING)
    own_cols = lax.dynamic_slice_in_dim(
        acts.astype(jnp.float32), lax.axis_index("dp") * ada_rows, ada_rows, 1
    )
    ada_grad = lax.dot_general(own_cols, grad_mod, (((0,), (0,)), ((), ())), precision=PRECISION)
    own_gain = jnp.sum(all_sums * factor, axis=0)
    own_extras = jnp.sum(gathered[:, SEGS], axis=0)
    last = jnp.stack(gather_tensor(jnp.stack([own_gain, own_extras])))
    norm_grads = jnp.stack([pick(last[:, 0], block) for block in order])
    extras_sum = jnp.sum(last[:, 1], axis=0)
    head_grads = extras_sum[: 3 * HEAD].reshape(3, HEAD)
    crossgate_grad = extras_sum[3 * HEAD : 3 * HEAD + HEADS]
    return (
        block_out,
        in_grad,
        ada_grad,
        norm_grads,
        query_sum,
        key_sum,
        value_sum,
        head_grads,
        textkey_sum,
        textvalue_sum,
        crossgate_grad,
        outw_sum.T,
        gate_sum,
        up_sum,
        down_sum,
    )


def solution(mesh):
    return jax.shard_map(
        shards,
        mesh=mesh,
        in_specs=(
            P(("dp", "tensor"), None),
            P(("dp", "tensor"), None),
            P("dp", None),
            P("dp", None, None),
            P("dp"),
            P("dp"),
            P(None, "tensor"),
            P(),
            P(None, "tensor"),
            P(None, "tensor"),
            P(None, "tensor"),
            P(),
            P(None, "tensor"),
            P(None, "tensor"),
            P("tensor"),
            P("tensor", None),
            P(None, "tensor"),
            P(None, "tensor"),
            P("tensor", None),
        ),
        out_specs=(
            P(("dp", "tensor"), None),
            P(("dp", "tensor"), None),
            P("dp", "tensor"),
            P(),
            P("dp", "tensor"),
            P("dp", "tensor"),
            P("dp", "tensor"),
            P(),
            P("dp", "tensor"),
            P("dp", "tensor"),
            P(),
            P("tensor", "dp"),
            P("dp", "tensor"),
            P("dp", "tensor"),
            P("tensor", "dp"),
        ),
        check_vma=False,
    )
```

time: 2660 us -> 562 us (0.21)
  waiting for transfers between devices: 2330 us -> 208 us
  starting transfers between devices: 1.54 us -> 87.6 us
  blocking collectives: 69.7 us -> 0 us
  local copies, waits for them, and re-layouts: 43.4 us -> 87.3 us
  matrix products: 126 us -> 96.3 us
    reduce_scatter x12 -> x0, waiting for transfers between devices: 1870 us -> none  [the longest x1 227 us: shards(): lax.psum_scatter(up_grad.astype(jnp.bfloat16), 'dp', scatter_dimension=0,...]
    unnamed x22 -> x0, waiting for transfers between devices: 385 us -> none
    ppermute x0 -> x81, waiting for transfers between devices: none -> 208 us  [the longest x39 138 us: scatter_stage(): lax.ppermute(sent, 'dp', dp_perm(axis, step)).astype(jnp.float32)]
    ppermute x0 -> x81, starting transfers between devices: none -> 87.6 us  [the longest x39 51.9 us: scatter_stage(): lax.ppermute(sent, 'dp', dp_perm(axis, step)).astype(jnp.float32)]
    all_gather x4 -> x0, waiting for transfers between devices: 75.3 us -> none  [the longest x1 25.9 us: shards(): lax.all_gather(ffn_in_f.astype(jnp.bfloat16), 'tensor', axis=0, tiled=True)]
    psum x1 -> x0, blocking collectives: 63.9 us -> none  [shards(): lax.psum((norm_stack, head_stack, gate_full), ('dp', 'tensor'))]
    dynamic_slice x1 -> x31, local copies, waits for them, and re-layouts: 0.07 us -> 30.9 us  [the longest x28 29.2 us: chunk_of(): lax.dynamic_index_in_dim(part, index, axis, keepdims=False)]
  transfers between devices with their start and end apart: 19 -> 81, of which waited for: 17 -> 32; matrix products, arithmetic and copies ran while one was open for 4% -> 28% of each run, Pallas kernels for 0% -> 0%
where the time goes in v1:
time: 562 us; the launch traced here: 552 us
  waiting for transfers between devices  208 us (37%)
  matrix products  96.3 us (17%)
  starting transfers between devices  87.6 us (16%)
  local copies, waits for them, and re-layouts  87.3 us (16%)
  other arithmetic  68 us (12%)
    ppermute x39, waiting for transfers between devices, scatter_stage(): lax.ppermute(sent, 'dp', dp_perm(axis, step)).astype(jnp.float32)  138 us
    ppermute x39, starting transfers between devices, scatter_stage(): lax.ppermute(sent, 'dp', dp_perm(axis, step)).astype(jnp.float32)  51.9 us
    ppermute x11, waiting for transfers between devices, swap_chip(): return lax.ppermute(values, 'tensor', CHIP_SWAP)  46 us
    unnamed x423, local copies, waits for them, and re-layouts  31.8 us
    dynamic_slice x28, local copies, waits for them, and re-layouts, chunk_of(): lax.dynamic_index_in_dim(part, index, axis, keepdims=False)  29.2 us
    dot_general x9, matrix products, contract_rows(): lax.dot_general(left, right, (((0,), (0,)), ((), ())), preferred_element_...  22.2 us
    ppermute x14, waiting for transfers between devices, gather_dp(): lax.ppermute(block, 'dp', dp_perm(axis, step))  21.8 us
    ppermute x14, starting transfers between devices, gather_dp(): lax.ppermute(block, 'dp', dp_perm(axis, step))  21.6 us
  transfers between devices with their start and end apart: 81, of which 32 were waited for; matrix products, arithmetic and copies ran while one was open for 28% of the time, Pallas kernels for 0%

profile of v1, /device:TPU:0, one launch (start us, length us, event | category | flops | bytes accessed | tf_op | source)
XLA Modules:
  0.0 551.7 jit_solution(10678719462083062094)
XLA Ops:
  12.1 4.7 copy.93
  16.8 7.5 %multiply_reduce_fusion.2 = (f32[768,6]{0,1:T(8,128)S(1)}, f32[768,6,64]{0,2,1:T(8,128)}) fusion(bf16[768,4096,1]{1,0,2:T(8,128)(2,1)} %bitcast.396, bf16[6,64,4096]{2,1,0:T(8,128)(2,1)} %bitcast.351), kind=kOutput, calls=%fused_computation.115 | convolution fusion | flops 2416504320 | bytes 10635264 | tf_op jit(solution)/shard_map/dot_general | solution.py:286
  26.5 6.3 %convolution_convert_fusion.11 = bf16[768,384]{0,1:T(8,128)(2,1)} fusion(bf16[768,4096]{1,0:T(8,128)(2,1)} %bitcast.397, bf16[4096,384]{1,0:T(8,128)(2,1)S(1)} %copy-done.175), kind=kOutput, calls=%fused_computation.78 | convolution fusion | flops 2416214016 | bytes 10027008 | tf_op jit(solution)/shard_map/dot_general | solution.py:289
  59.8 3.8 fusion.37
  71.4 9.4 %collective-permute-done.7 = bf16[128,1536]{1,0:T(8,128)(2,1)S(1)} collective-permute-done((bf16[128,1536]{1,0:T(8,128)(2,1)S(1)}, bf16[128,1536]{1,0:T(8,128)(2,1)S(1)}, u32[]{:S(2)}, u32[]{:S(2)}) %collective-permute-start.7) | collective-permute-done | bytes 393248 | tf_op jit(solution)/shard_map/ppermute | solution.py:49
  85.2 8.9 %collective-permute-done.9 = bf16[128,1536]{1,0:T(8,128)(2,1)S(1)} collective-permute-done((bf16[128,1536]{1,0:T(8,128)(2,1)S(1)}, bf16[128,1536]{1,0:T(8,128)(2,1)S(1)}, u32[]{:S(2)}, u32[]{:S(2)}) %collective-permute-start.9) | collective-permute-done | bytes 393248 | tf_op jit(solution)/shard_map/ppermute | solution.py:49
  143.5 6.6 %collective-permute-done.14 = bf16[128,1536]{1,0:T(8,128)(2,1)S(1)} collective-permute-done((bf16[128,1536]{1,0:T(8,128)(2,1)S(1)}, bf16[128,1536]{1,0:T(8,128)(2,1)S(1)}, u32[]{:S(2)}, u32[]{:S(2)}) %collective-permute-start.14) | collective-permute-done | bytes 393248 | tf_op jit(solution)/shard_map/ppermute | solution.py:49
  177.0 9.8 %collective-permute-done.17 = bf16[128,1536]{1,0:T(8,128)(2,1)S(1)} collective-permute-done((bf16[128,1536]{1,0:T(8,128)(2,1)S(1)}, bf16[128,1536]{1,0:T(8,128)(2,1)S(1)}, u32[]{:S(2)}, u32[]{:S(2)}) %collective-permute-start.17) | collective-permute-done | bytes 393248 | tf_op jit(solution)/shard_map/ppermute | solution.py:49
  191.1 27.3 %collective-permute-done.74 = bf16[4,2,48,1536]{3,2,1,0:T(8,128)(2,1)S(1)} collective-permute-done((bf16[4,2,48,1536]{3,2,1,0:T(8,128)(2,1)S(1)}, bf16[4,2,48,1536]{3,2,1,0:T(8,128)(2,1)S(1)}, u32[]{:S(2)}, u32[]{:S(2)}) %collective-permute-start.74) | collective-permute-done | bytes 1179680 | tf_op jit(solution)/shard_map/ppermute | solution.py:99
  222.3 7.6 %collective-permute-done.68 = bf16[2,4,48,1536]{3,2,0,1:T(8,128)(2,1)S(1)} collective-permute-done((bf16[2,4,48,1536]{3,2,0,1:T(8,128)(2,1)S(1)}, bf16[2,4,48,1536]{3,2,0,1:T(8,128)(2,1)S(1)}, u32[]{:S(2)}, u32[]{:S(2)}) %collective-permute-start.68) | collective-permute-done | bytes 1179680 | tf_op jit(solution)/shard_map/ppermute | solution.py:99
  233.1 14.1 %collective-permute-done.70 = bf16[2,4,48,1536]{3,2,0,1:T(8,128)(2,1)S(1)} collective-permute-done((bf16[2,4,48,1536]{3,2,0,1:T(8,128)(2,1)S(1)}, bf16[2,4,48,1536]{3,2,0,1:T(8,128)(2,1)S(1)}, u32[]{:S(2)}, u32[]{:S(2)}) %collective-permute-start.70) | collective-permute-done | bytes 1179680 | tf_op jit(solution)/shard_map/ppermute | solution.py:99
  257.8 10.7 %collective-permute-done.73 = bf16[2,48,1536]{2,1,0:T(8,128)(2,1)S(1)} collective-permute-done((bf16[2,48,1536]{2,1,0:T(8,128)(2,1)S(1)}, bf16[2,48,1536]{2,1,0:T(8,128)(2,1)S(1)}, u32[]{:S(2)}, u32[]{:S(2)}) %collective-permute-start.73) | collective-permute-done | bytes 294944 | tf_op jit(solution)/shard_map/ppermute | solution.py:99
  272.7 5.2 collective-permute-done.80
  281.8 4.0 multiply_reduce_fusion.1
  285.8 4.8 multiply_convert_fusion.1
  319.2 4.3 collective-permute-start.49
  324.4 4.5 fusion.4
  328.9 4.7 reshape.556
  344.2 6.1 %collective-permute-start.43 = (bf16[2,4,48,768]{3,2,0,1:T(8,128)(2,1)}, bf16[2,4,48,768]{3,2,0,1:T(8,128)(2,1)}, u32[]{:S(2)}, u32[]{:S(2)}) collective-permute-start(bf16[2,4,48,768]{3,2,0,1:T(8,128)(2,1)} %pad_maximum_fusion.15), channel_id=1, source_target_pairs={{0,64},{4,68},{8,72},{12,76},{16,80},{20,84},{24,88},{28,92},{32,9... | collective-permute-start | bytes 1769480 | tf_op jit(solution)/shard_map/ppermute | solution.py:99
  350.3 7.0 %fusion.3 = bf16[4096,384]{0,1:T(8,128)(2,1)} fusion(bf16[768,384]{0,1:T(8,128)(2,1)S(1)} %bitcast.386, bf16[768,4096]{1,0:T(8,128)(2,1)} %bitcast.398), kind=kOutput, calls=%fused_computation.17 | convolution fusion | flops 2417491968 | bytes 10027008 | tf_op jit(solution)/shard_map/dot_general | solution.py:53
  361.9 7.7 %constant_dynamic-slice_fusion.18 = (bf16[4,2,1,128,384]{3,2,1,0,4:T(2,128)(2,1)}, bf16[4,2,1,128,384]{3,2,1,0,4:T(2,128)(2,1)}, bf16[4,2,1,128,384]{3,2,1,0,4:T(2,128)(2,1)}, bf16[4,2,1,128,384]{3,2,1,0,4:T(2,128)(2,1)}) fusion(bf16[4,2,4,128,384]{3,2,1,0,4:T(4,128)(2,1)S(1)} %reshape.556, s32[]{:T(128)S(6)} %select_n.376, s32[]{:T(128)S(6)} %select_n.382, ...), kind=kLoop, calls=%fused_computation.366 | loop fusion | bytes 6291472 | tf_op jit(solution)/shard_map/jit(dynamic_index_in_dim)/dynamic_slice | solution.py:114
  369.6 4.7 copy.113
  374.2 4.7 reshape.555
  391.5 7.0 %collective-permute-done.44 = bf16[2,4,48,768]{3,2,0,1:T(8,128)(2,1)S(1)} collective-permute-done((bf16[2,4,48,768]{3,2,0,1:T(8,128)(2,1)S(1)}, bf16[2,4,48,768]{3,2,0,1:T(8,128)(2,1)S(1)}, u32[]{:S(2)}, u32[]{:S(2)}) %collective-permute-start.44) | collective-permute-done | bytes 589856 | tf_op jit(solution)/shard_map/ppermute | solution.py:99
  405.3 4.9 copy.129
  427.5 23.2 %collective-permute-done.47 = bf16[2,48,768]{2,1,0:T(8,128)(2,1)S(1)} collective-permute-done((bf16[2,48,768]{2,1,0:T(8,128)(2,1)}, bf16[2,48,768]{2,1,0:T(8,128)(2,1)S(1)}, u32[]{:S(2)}, u32[]{:S(2)}) %collective-permute-start.47) | collective-permute-done | bytes 147488 | tf_op jit(solution)/shard_map/ppermute | solution.py:99
  457.5 15.2 %collective-permute-done.55 = bf16[2,4,128,384]{3,2,0,1:T(8,128)(2,1)S(1)} collective-permute-done((bf16[2,4,128,384]{3,2,0,1:T(8,128)(2,1)}, bf16[2,4,128,384]{3,2,0,1:T(8,128)(2,1)S(1)}, u32[]{:S(2)}, u32[]{:S(2)}) %collective-permute-start.55) | collective-permute-done | bytes 786464 | tf_op jit(solution)/shard_map/ppermute | solution.py:99
  472.7 16.9 %collective-permute-done.56 = bf16[2,4,128,384]{3,2,0,1:T(8,128)(2,1)S(1)} collective-permute-done((bf16[2,4,128,384]{3,2,0,1:T(8,128)(2,1)}, bf16[2,4,128,384]{3,2,0,1:T(8,128)(2,1)S(1)}, u32[]{:S(2)}, u32[]{:S(2)}) %collective-permute-start.56) | collective-permute-done | bytes 786464 | tf_op jit(solution)/shard_map/ppermute | solution.py:99
  503.0 4.0 collective-permute-done.22
  513.2 5.3 collective-permute-done.32
  523.3 5.3 collective-permute-done.33
  532.2 4.0 collective-permute-done.36
  (793 shorter events, 287.8 us)
Async XLA Ops:
  3.9 30.6 %collective-permute-start.1 = (f32[3,1536]{1,0:T(4,128)}, f32[3,1536]{1,0:T(4,128)}, u32[]{:S(2)}, u32[]{:S(2)}) collective-permute-start(f32[3,1536]{1,0:T(4,128)} %fusion.134), channel_id=1, source_target_pairs={{0,2},{2,0},{1,3},{3,1},{4,6},{6,4},{5,7},{7,5},{8,10},{10,8},{9,1... | collective-permute-start | bytes 55304 | tf_op jit(solution)/shard_map/ppermute | solution.py:49
  5.9 32.0 %collective-permute-start = (f32[3,1536]{1,0:T(4,128)}, f32[3,1536]{1,0:T(4,128)}, u32[]{:S(2)}, u32[]{:S(2)}) collective-permute-start(f32[3,1536]{1,0:T(4,128)} %fusion.134), channel_id=1, source_target_pairs={{0,1},{1,0},{2,3},{3,2},{4,5},{5,4},{6,7},{7,6},{8,9},{9,8},{10,11... | collective-permute-start | bytes 55304 | tf_op jit(solution)/shard_map/ppermute | solution.py:45
  5.9 33.6 %collective-permute-start.3 = (bf16[128,1536]{1,0:T(8,128)(2,1)S(1)}, bf16[128,1536]{1,0:T(8,128)(2,1)}, u32[]{:S(2)}, u32[]{:S(2)}) collective-permute-start(bf16[128,1536]{1,0:T(8,128)(2,1)S(1)} %copy-done.18), channel_id=1, source_target_pairs={{0,1},{1,0},{2,3},{3,2},{4,5},{5,4},{6,7},{7,6},{8,9},{9,8},{10,11... | collective-permute-start | bytes 1179656 | tf_op jit(solution)/shard_map/ppermute | solution.py:45
  6.4 28.0 %collective-permute-start.4 = (bf16[128,1536]{1,0:T(8,128)(2,1)S(1)}, bf16[128,1536]{1,0:T(8,128)(2,1)}, u32[]{:S(2)}, u32[]{:S(2)}) collective-permute-start(bf16[128,1536]{1,0:T(8,128)(2,1)S(1)} %copy-done.18), channel_id=1, source_target_pairs={{0,2},{2,0},{1,3},{3,1},{4,6},{6,4},{5,7},{7,5},{8,10},{10,8},{9,1... | collective-permute-start | bytes 1179656 | tf_op jit(solution)/shard_map/ppermute | solution.py:49
  163.4 54.9 %collective-permute-start.74 = (bf16[4,2,48,1536]{3,2,1,0:T(8,128)(2,1)S(1)}, bf16[4,2,48,1536]{3,2,1,0:T(8,128)(2,1)S(1)}, u32[]{:S(2)}, u32[]{:S(2)}) collective-permute-start(bf16[4,2,48,1536]{3,2,1,0:T(8,128)(2,1)S(1)} %pad_maximum_fusion.7), channel_id=1, source_target_pairs={{0,4},{4,8},{8,12},{12,0},{16,20},{20,24},{24,28},{28,16},{32,36},... | collective-permute-start | bytes 3538952 | tf_op jit(solution)/shard_map/ppermute | solution.py:99
  163.7 56.8 %collective-permute-start.75 = (bf16[4,2,48,1536]{3,2,1,0:T(8,128)(2,1)S(1)}, bf16[4,2,48,1536]{3,2,1,0:T(8,128)(2,1)S(1)}, u32[]{:S(2)}, u32[]{:S(2)}) collective-permute-start(bf16[4,2,48,1536]{3,2,1,0:T(8,128)(2,1)S(1)} %pad_maximum_fusion.8), channel_id=1, source_target_pairs={{0,8},{4,12},{8,0},{12,4},{16,24},{20,28},{24,16},{28,20},{32,40},... | collective-permute-start | bytes 3538952 | tf_op jit(solution)/shard_map/ppermute | solution.py:99
  166.5 55.1 %collective-permute-start.76 = (bf16[4,2,48,1536]{3,2,1,0:T(8,128)(2,1)S(1)}, bf16[4,2,48,1536]{3,2,1,0:T(8,128)(2,1)S(1)}, u32[]{:S(2)}, u32[]{:S(2)}) collective-permute-start(bf16[4,2,48,1536]{3,2,1,0:T(8,128)(2,1)S(1)} %pad_maximum_fusion.9), channel_id=1, source_target_pairs={{0,12},{4,0},{8,4},{12,8},{16,28},{20,16},{24,20},{28,24},{32,44},... | collective-permute-start | bytes 3538952 | tf_op jit(solution)/shard_map/ppermute | solution.py:99
  175.0 54.8 %collective-permute-start.68 = (bf16[2,4,48,1536]{3,2,0,1:T(8,128)(2,1)S(1)}, bf16[2,4,48,1536]{3,2,0,1:T(8,128)(2,1)S(1)}, u32[]{:S(2)}, u32[]{:S(2)}) collective-permute-start(bf16[2,4,48,1536]{3,2,0,1:T(8,128)(2,1)S(1)} %pad_maximum_fusion.4), channel_id=1, source_target_pairs={{0,32},{4,36},{8,40},{12,44},{16,48},{20,52},{24,56},{28,60},{32,6... | collective-permute-start | bytes 3538952 | tf_op jit(solution)/shard_map/ppermute | solution.py:99
  186.8 43.4 %collective-permute-start.69 = (bf16[2,4,48,1536]{3,2,0,1:T(8,128)(2,1)S(1)}, bf16[2,4,48,1536]{3,2,0,1:T(8,128)(2,1)S(1)}, u32[]{:S(2)}, u32[]{:S(2)}) collective-permute-start(bf16[2,4,48,1536]{3,2,0,1:T(8,128)(2,1)S(1)} %pad_maximum_fusion.5), channel_id=1, source_target_pairs={{0,64},{4,68},{8,72},{12,76},{16,80},{20,84},{24,88},{28,92},{32,9... | collective-permute-start | bytes 3538952 | tf_op jit(solution)/shard_map/ppermute | solution.py:99
  218.4 28.9 %collective-permute-start.70 = (bf16[2,4,48,1536]{3,2,0,1:T(8,128)(2,1)S(1)}, bf16[2,4,48,1536]{3,2,0,1:T(8,128)(2,1)S(1)}, u32[]{:S(2)}, u32[]{:S(2)}) collective-permute-start(bf16[2,4,48,1536]{3,2,0,1:T(8,128)(2,1)S(1)} %pad_maximum_fusion.6), channel_id=1, source_target_pairs={{0,96},{4,100},{8,104},{12,108},{16,112},{20,116},{24,120},{28,124... | collective-permute-start | bytes 3538952 | tf_op jit(solution)/shard_map/ppermute | solution.py:99
  220.4 52.1 %collective-permute-start.19 = (bf16[128,1536]{1,0:T(8,128)(2,1)S(1)}, bf16[128,1536]{1,0:T(8,128)(2,1)S(1)}, u32[]{:S(2)}, u32[]{:S(2)}) collective-permute-start(bf16[128,1536]{1,0:T(8,128)(2,1)S(1)} %multiply_convert_fusion.6), channel_id=1, source_target_pairs={{0,2},{2,0},{1,3},{3,1},{4,6},{6,4},{5,7},{7,5},{8,10},{10,8},{9,1... | collective-permute-start | bytes 1179656 | tf_op jit(solution)/shard_map/ppermute | solution.py:49
  221.5 57.3 %collective-permute-start.18 = (bf16[128,1536]{1,0:T(8,128)(2,1)S(1)}, bf16[128,1536]{1,0:T(8,128)(2,1)S(1)}, u32[]{:S(2)}, u32[]{:S(2)}) collective-permute-start(bf16[128,1536]{1,0:T(8,128)(2,1)S(1)} %multiply_convert_fusion.6), channel_id=1, source_target_pairs={{0,1},{1,0},{2,3},{3,2},{4,5},{5,4},{6,7},{7,6},{8,9},{9,8},{10,11... | collective-permute-start | bytes 1179656 | tf_op jit(solution)/shard_map/ppermute | solution.py:45
  230.2 23.4 %collective-permute-start.79 = (bf16[2,48,1536]{2,1,0:T(8,128)(2,1)S(1)}, bf16[2,48,1536]{2,1,0:T(8,128)(2,1)S(1)}, u32[]{:S(2)}, u32[]{:S(2)}) collective-permute-start(bf16[2,48,1536]{2,1,0:T(8,128)(2,1)S(1)} %get-tuple-element.87), channel_id=1, source_target_pairs={{0,96},{4,100},{8,104},{12,108},{16,112},{20,116},{24,120},{28,124... | collective-permute-start | bytes 884744 | tf_op jit(solution)/shard_map/ppermute | solution.py:99
  317.5 65.0 %collective-permute-start.48 = (bf16[4,2,48,768]{3,2,1,0:T(8,128)(2,1)}, bf16[4,2,48,768]{3,2,1,0:T(8,128)(2,1)}, u32[]{:S(2)}, u32[]{:S(2)}) collective-permute-start(bf16[4,2,48,768]{3,2,1,0:T(8,128)(2,1)} %pad_maximum_fusion.17), channel_id=1, source_target_pairs={{0,4},{4,8},{8,12},{12,0},{16,20},{20,24},{24,28},{28,16},{32,36},... | collective-permute-start | bytes 1769480 | tf_op jit(solution)/shard_map/ppermute | solution.py:99
  319.2 63.4 %collective-permute-start.49 = (bf16[4,2,48,768]{3,2,1,0:T(8,128)(2,1)}, bf16[4,2,48,768]{3,2,1,0:T(8,128)(2,1)}, u32[]{:S(2)}, u32[]{:S(2)}) collective-permute-start(bf16[4,2,48,768]{3,2,1,0:T(8,128)(2,1)} %pad_maximum_fusion.18), channel_id=1, source_target_pairs={{0,8},{4,12},{8,0},{12,4},{16,24},{20,28},{24,16},{28,20},{32,40},... | collective-permute-start | bytes 1769480 | tf_op jit(solution)/shard_map/ppermute | solution.py:99
  324.4 60.2 %collective-permute-start.50 = (bf16[4,2,48,768]{3,2,1,0:T(8,128)(2,1)}, bf16[4,2,48,768]{3,2,1,0:T(8,128)(2,1)}, u32[]{:S(2)}, u32[]{:S(2)}) collective-permute-start(bf16[4,2,48,768]{3,2,1,0:T(8,128)(2,1)} %pad_maximum_fusion.19), channel_id=1, source_target_pairs={{0,12},{4,0},{8,4},{12,8},{16,28},{20,16},{24,20},{28,24},{32,44},... | collective-permute-start | bytes 1769480 | tf_op jit(solution)/shard_map/ppermute | solution.py:99
  343.4 46.0 %collective-permute-start.42 = (bf16[2,4,48,768]{3,2,0,1:T(8,128)(2,1)}, bf16[2,4,48,768]{3,2,0,1:T(8,128)(2,1)}, u32[]{:S(2)}, u32[]{:S(2)}) collective-permute-start(bf16[2,4,48,768]{3,2,0,1:T(8,128)(2,1)} %pad_maximum_fusion.14), channel_id=1, source_target_pairs={{0,32},{4,36},{8,40},{12,44},{16,48},{20,52},{24,56},{28,60},{32,6... | collective-permute-start | bytes 1769480 | tf_op jit(solution)/shard_map/ppermute | solution.py:99
  344.2 46.4 %collective-permute-start.43 = (bf16[2,4,48,768]{3,2,0,1:T(8,128)(2,1)}, bf16[2,4,48,768]{3,2,0,1:T(8,128)(2,1)}, u32[]{:S(2)}, u32[]{:S(2)}) collective-permute-start(bf16[2,4,48,768]{3,2,0,1:T(8,128)(2,1)} %pad_maximum_fusion.15), channel_id=1, source_target_pairs={{0,64},{4,68},{8,72},{12,76},{16,80},{20,84},{24,88},{28,92},{32,9... | collective-permute-start | bytes 1769480 | tf_op jit(solution)/shard_map/ppermute | solution.py:99
  382.6 71.4 %collective-permute-start.61 = (bf16[4,2,128,384]{3,2,1,0:T(8,128)(2,1)}, bf16[4,2,128,384]{3,2,1,0:T(8,128)(2,1)}, u32[]{:S(2)}, u32[]{:S(2)}) collective-permute-start(bf16[4,2,128,384]{3,2,1,0:T(8,128)(2,1)} %bitcast.88), channel_id=1, source_target_pairs={{0,4},{4,8},{8,12},{12,0},{16,20},{20,24},{24,28},{28,16},{32,36},... | collective-permute-start | bytes 2359304 | tf_op jit(solution)/shard_map/ppermute | solution.py:99
  387.2 28.5 %collective-permute-start.51 = (bf16[2,48,768]{2,1,0:T(8,128)(2,1)}, bf16[2,48,768]{2,1,0:T(8,128)(2,1)S(1)}, u32[]{:S(2)}, u32[]{:S(2)}) collective-permute-start(bf16[2,48,768]{2,1,0:T(8,128)(2,1)} %get-tuple-element.126), channel_id=1, source_target_pairs={{0,32},{4,36},{8,40},{12,44},{16,48},{20,52},{24,56},{28,60},{32,6... | collective-permute-start | bytes 442376 | tf_op jit(solution)/shard_map/ppermute | solution.py:99
  389.4 26.7 %collective-permute-start.53 = (bf16[2,48,768]{2,1,0:T(8,128)(2,1)}, bf16[2,48,768]{2,1,0:T(8,128)(2,1)}, u32[]{:S(2)}, u32[]{:S(2)}) collective-permute-start(bf16[2,48,768]{2,1,0:T(8,128)(2,1)} %get-tuple-element.127), channel_id=1, source_target_pairs={{0,96},{4,100},{8,104},{12,108},{16,112},{20,116},{24,120},{28,124... | collective-permute-start | bytes 442376 | tf_op jit(solution)/shard_map/ppermute | solution.py:99
  390.6 33.9 %collective-permute-start.52 = (bf16[2,48,768]{2,1,0:T(8,128)(2,1)}, bf16[2,48,768]{2,1,0:T(8,128)(2,1)}, u32[]{:S(2)}, u32[]{:S(2)}) collective-permute-start(bf16[2,48,768]{2,1,0:T(8,128)(2,1)} %get-tuple-element.128), channel_id=1, source_target_pairs={{0,64},{4,68},{8,72},{12,76},{16,80},{20,84},{24,88},{28,92},{32,9... | collective-permute-start | bytes 442376 | tf_op jit(solution)/shard_map/ppermute | solution.py:99
  401.0 24.9 %collective-permute-start.45 = (bf16[2,48,768]{2,1,0:T(8,128)(2,1)}, bf16[2,48,768]{2,1,0:T(8,128)(2,1)S(1)}, u32[]{:S(2)}, u32[]{:S(2)}) collective-permute-start(bf16[2,48,768]{2,1,0:T(8,128)(2,1)} %get-tuple-element.129), channel_id=1, source_target_pairs={{0,4},{4,8},{8,12},{12,0},{16,20},{20,24},{24,28},{28,16},{32,36},... | collective-permute-start | bytes 442376 | tf_op jit(solution)/shard_map/ppermute | solution.py:99
  415.7 39.4 %collective-permute-start.62 = (bf16[4,2,128,384]{3,2,1,0:T(8,128)(2,1)}, bf16[4,2,128,384]{3,2,1,0:T(8,128)(2,1)}, u32[]{:S(2)}, u32[]{:S(2)}) collective-permute-start(bf16[4,2,128,384]{3,2,1,0:T(8,128)(2,1)} %bitcast.383), channel_id=1, source_target_pairs={{0,8},{4,12},{8,0},{12,4},{16,24},{20,28},{24,16},{28,20},{32,40},... | collective-permute-start | bytes 2359304 | tf_op jit(solution)/shard_map/ppermute | solution.py:99
  416.0 39.2 %collective-permute-start.63 = (bf16[4,2,128,384]{3,2,1,0:T(8,128)(2,1)}, bf16[4,2,128,384]{3,2,1,0:T(8,128)(2,1)}, u32[]{:S(2)}, u32[]{:S(2)}) collective-permute-start(bf16[4,2,128,384]{3,2,1,0:T(8,128)(2,1)} %bitcast.382), channel_id=1, source_target_pairs={{0,12},{4,0},{8,4},{12,8},{16,28},{20,16},{24,20},{28,24},{32,44},... | collective-permute-start | bytes 2359304 | tf_op jit(solution)/shard_map/ppermute | solution.py:99
  424.5 26.3 %collective-permute-start.47 = (bf16[2,48,768]{2,1,0:T(8,128)(2,1)}, bf16[2,48,768]{2,1,0:T(8,128)(2,1)S(1)}, u32[]{:S(2)}, u32[]{:S(2)}) collective-permute-start(bf16[2,48,768]{2,1,0:T(8,128)(2,1)} %get-tuple-element.130), channel_id=1, source_target_pairs={{0,12},{4,0},{8,4},{12,8},{16,28},{20,16},{24,20},{28,24},{32,44},... | collective-permute-start | bytes 442376 | tf_op jit(solution)/shard_map/ppermute | solution.py:99
  425.9 24.8 %collective-permute-start.46 = (bf16[2,48,768]{2,1,0:T(8,128)(2,1)S(1)}, bf16[2,48,768]{2,1,0:T(8,128)(2,1)S(1)}, u32[]{:S(2)}, u32[]{:S(2)}) collective-permute-start(bf16[2,48,768]{2,1,0:T(8,128)(2,1)S(1)} %copy-done.98), channel_id=1, source_target_pairs={{0,8},{4,12},{8,0},{12,4},{16,24},{20,28},{24,16},{28,20},{32,40},... | collective-permute-start | bytes 442376 | tf_op jit(solution)/shard_map/ppermute | solution.py:99
  450.8 38.8 %collective-permute-start.56 = (bf16[2,4,128,384]{3,2,0,1:T(8,128)(2,1)}, bf16[2,4,128,384]{3,2,0,1:T(8,128)(2,1)S(1)}, u32[]{:S(2)}, u32[]{:S(2)}) collective-permute-start(bf16[2,4,128,384]{3,2,0,1:T(8,128)(2,1)} %bitcast.380), channel_id=1, source_target_pairs={{0,64},{4,68},{8,72},{12,76},{16,80},{20,84},{24,88},{28,92},{32,9... | collective-permute-start | bytes 2359304 | tf_op jit(solution)/shard_map/ppermute | solution.py:99
  454.0 35.6 %collective-permute-start.57 = (bf16[2,4,128,384]{3,2,0,1:T(8,128)(2,1)S(1)}, bf16[2,4,128,384]{3,2,0,1:T(8,128)(2,1)S(1)}, u32[]{:S(2)}, u32[]{:S(2)}) collective-permute-start(bf16[2,4,128,384]{3,2,0,1:T(8,128)(2,1)S(1)} %bitcast.379), channel_id=1, source_target_pairs={{0,96},{4,100},{8,104},{12,108},{16,112},{20,116},{24,120},{28,124... | collective-permute-start | bytes 2359304 | tf_op jit(solution)/shard_map/ppermute | solution.py:99
  455.1 35.4 %collective-permute-start.21 = (bf16[256,1536]{1,0:T(8,128)(2,1)}, bf16[256,1536]{1,0:T(8,128)(2,1)S(1)}, u32[]{:S(2)}, u32[]{:S(2)}) collective-permute-start(bf16[256,1536]{1,0:T(8,128)(2,1)} %pad_maximum_fusion.13), channel_id=1, source_target_pairs={{0,1},{1,0},{2,3},{3,2},{4,5},{5,4},{6,7},{7,6},{8,9},{9,8},{10,11... | collective-permute-start | bytes 2359304 | tf_op jit(solution)/shard_map/ppermute | solution.py:45
  455.2 37.4 %collective-permute-start.54 = (bf16[48,1536]{1,0:T(8,128)(2,1)S(1)}, bf16[48,1536]{1,0:T(8,128)(2,1)S(1)}, u32[]{:S(2)}, u32[]{:S(2)}) collective-permute-start(bf16[48,1536]{1,0:T(8,128)(2,1)S(1)} %fusion.114), channel_id=1, source_target_pairs={{0,16},{4,20},{8,24},{12,28},{16,0},{20,4},{24,8},{28,12},{32,48},... | collective-permute-start | bytes 442376 | tf_op jit(solution)/shard_map/ppermute | solution.py:99
  502.7 27.3 %collective-permute-start.67 = (bf16[128,768]{1,0:T(8,128)(2,1)S(1)}, bf16[128,768]{1,0:T(8,128)(2,1)S(1)}, u32[]{:S(2)}, u32[]{:S(2)}) collective-permute-start(bf16[128,768]{1,0:T(8,128)(2,1)S(1)} %fusion.110), channel_id=1, source_target_pairs={{0,16},{4,20},{8,24},{12,28},{16,0},{20,4},{24,8},{28,12},{32,48},... | collective-permute-start | bytes 589832 | tf_op jit(solution)/shard_map/ppermute | solution.py:99
  (253 other events, 2249.2 us)

commit v2 on v1

--- a/solution.py
+++ b/solution.py
@@ -1,8 +1,11 @@
+import functools
 import math
 
 import jax
 import jax.numpy as jnp
 from jax import lax
+from jax.experimental import pallas as pl
+from jax.experimental.pallas import tpu as pltpu
 from jax.sharding import PartitionSpec as P
 
 HEAD = 64
@@ -67,15 +70,16 @@
     return [block, near, far, swap_core(far)]
 
 
-def scatter_tensor(blocks):
+def scatter_tensor(blocks, with_sent=False):
     near = swap_core(jnp.concatenate([blocks[1], blocks[3]], axis=0))
     rows = blocks[0].shape[0]
     far = (blocks[2].astype(jnp.float32) + near[rows:].astype(jnp.float32)).astype(near.dtype)
-    return (
+    total = (
         blocks[0].astype(jnp.float32)
         + near[:rows].astype(jnp.float32)
         + swap_chip(far).astype(jnp.float32)
     )
+    return (total, far) if with_sent else total
 
 
 def pick(stacked, index):
@@ -92,41 +96,263 @@
     return block
 
 
-def scatter_stage(chunk_of, axis, place, size):
-    total = chunk_of(place).astype(jnp.float32)
-    for step in range(1, size):
-        sent = chunk_of((place + step) % size)
-        total = total + lax.ppermute(sent, "dp", dp_perm(axis, step)).astype(jnp.float32)
+BLOCKS = RING * PAIR * RING
+SLOTS = BLOCKS // RING
+SEND_ORDER = (2, 1, 3, 0)
+VMEM_LIMIT = 50 * 2**20
+
+
+def turn_kernel(source, target):
+    target[...] = source[...].T
+
+
+def turned(values, ties=()):
+    tile = 512 if values.shape[1] % 512 == 0 else values.shape[1]
+    return pl.pallas_call(
+        lambda source, *rest: turn_kernel(source, rest[-1]),
+        grid=(values.shape[1] // tile,),
+        in_specs=[pl.BlockSpec((values.shape[0], tile), lambda step: (0, step))]
+        + [pl.BlockSpec(memory_space=pl.ANY)] * len(ties),
+        out_specs=pl.BlockSpec((tile, values.shape[0]), lambda step: (step, 0)),
+        out_shape=jax.ShapeDtypeStruct(values.shape[::-1], values.dtype),
+        compiler_params=pltpu.CompilerParams(vmem_limit_bytes=VMEM_LIMIT),
+        cost_estimate=pl.CostEstimate(
+            flops=0, bytes_accessed=4 * values.size, transcendentals=0
+        ),
+    )(values, *ties)
+
+
+def send_chunk(step, make, outs, held, sems):
+    def copy(place):
+        return pltpu.make_async_copy(
+            held.at[place % 2], outs[SEND_ORDER[place]], sems.at[place % 2]
+        )
+
+    for place in range(RING):
+
+        @pl.when(step == place)
+        def _(place=place):
+            if place >= 2:
+                copy(place - 2).wait()
+            make(held.at[place % 2])
+            copy(place).start()
+            if place == RING - 1:
+                copy(place - 1).wait()
+                copy(place).wait()
+
+
+def chunk_of_step(step, here):
+    offset = jnp.where(step == 0, 2, jnp.where(step == 1, 1, jnp.where(step == 2, 3, 0)))
+    return (here[0] + offset) % RING
+
+
+def row_chunk_kernel(pairs, here, *refs):
+    lefts, rights = refs[:pairs], refs[pairs : 2 * pairs]
+    outs, held, sems = refs[-RING - 2 : -2], refs[-2], refs[-1]
+
+    def make(slot):
+        column = 0
+        for left, right in zip(lefts, rights):
+            rows = left[...].reshape(-1, left.shape[-1])
+            product = jnp.dot(rows, right[...], preferred_element_type=jnp.float32)
+            slot[:, column : column + right.shape[1]] = product.astype(jnp.bfloat16)
+            column += right.shape[1]
+
+    send_chunk(pl.program_id(0), make, outs, held, sems)
+
+
+def row_chunks(pairs, axis, place, ties=()):
+    lefts = [
+        left.reshape(RING, PAIR, RING, left.shape[0] // BLOCKS, left.shape[1])
+        for left, _ in pairs
+    ]
+    rights = [right for _, right in pairs]
+    rows = lefts[0].shape[3]
+    total = sum(right.shape[1] for right in rights)
+
+    def spec(left):
+        if axis == "x":
+            return pl.BlockSpec(
+                (1, PAIR, RING, rows, left.shape[-1]),
+                lambda step, here: (chunk_of_step(step, here), 0, 0, 0, 0),
+            )
+        return pl.BlockSpec(
+            (RING, PAIR, 1, rows, left.shape[-1]),
+            lambda step, here: (0, 0, chunk_of_step(step, here), 0, 0),
+        )
+
+    return pl.pallas_call(
+        functools.partial(row_chunk_kernel, len(pairs)),
+        grid_spec=pltpu.PrefetchScalarGridSpec(
+            num_scalar_prefetch=1,
+            grid=(RING,),
+            in_specs=[spec(left) for left in lefts]
+            + [pl.BlockSpec(right.shape, lambda step, here: (0, 0)) for right in rights]
+            + [pl.BlockSpec(memory_space=pl.ANY)] * len(ties),
+            out_specs=[pl.BlockSpec(memory_space=pl.ANY)] * RING,
+            scratch_shapes=[
+                pltpu.VMEM((2, SLOTS * rows, total), jnp.bfloat16),
+                pltpu.SemaphoreType.DMA((2,)),
+            ],
+        ),
+        out_shape=[jax.ShapeDtypeStruct((SLOTS * rows, total), jnp.bfloat16)] * RING,
+        compiler_params=pltpu.CompilerParams(vmem_limit_bytes=VMEM_LIMIT),
+        cost_estimate=pl.CostEstimate(
+            flops=sum(2 * left.size * right.shape[1] for left, right in zip(lefts, rights)),
+            bytes_accessed=2 * sum(part.size for part in lefts + rights)
+            + 2 * BLOCKS * rows * total,
+            transcendentals=0,
+        ),
+    )(place[axis].reshape(1), *lefts, *rights, *ties)
+
+
+def column_chunk_kernel(pieces, here, left, *refs):
+    rights = refs[:pieces]
+    outs, held, sems = refs[-RING - 2 : -2], refs[-2], refs[-1]
+
+    def make(slot):
+        lanes = rights[0].shape[1]
+        for piece, right in enumerate(rights):
+            product = jnp.dot(left[...], right[...], preferred_element_type=jnp.float32)
+            slot[:, piece * lanes : (piece + 1) * lanes] = product.astype(jnp.bfloat16)
+
+    send_chunk(pl.program_id(0), make, outs, held, sems)
+
+
+def column_chunks(left, right, axis, place, ties=()):
+    rows, depth = left.shape
+    columns = right.shape[1]
+    if axis == "x":
+        specs = [
+            pl.BlockSpec(
+                (depth, columns // RING), lambda step, here: (0, chunk_of_step(step, here))
+            )
+        ]
+    else:
+        specs = [
+            pl.BlockSpec(
+                (depth, columns // BLOCKS),
+                lambda step, here, slot=slot: (0, slot * RING + chunk_of_step(step, here)),
+            )
+            for slot in range(SLOTS)
+        ]
+    return pl.pallas_call(
+        functools.partial(column_chunk_kernel, len(specs)),
+        grid_spec=pltpu.PrefetchScalarGridSpec(
+            num_scalar_prefetch=1,
+            grid=(RING,),
+            in_specs=[pl.BlockSpec((rows, depth), lambda step, here: (0, 0))]
+            + specs
+            + [pl.BlockSpec(memory_space=pl.ANY)] * len(ties),
+            out_specs=[pl.BlockSpec(memory_space=pl.ANY)] * RING,
+            scratch_shapes=[
+                pltpu.VMEM((2, rows, columns // RING), jnp.bfloat16),
+                pltpu.SemaphoreType.DMA((2,)),
+            ],
+        ),
+        out_shape=[jax.ShapeDtypeStruct((rows, columns // RING), jnp.bfloat16)] * RING,
+        compiler_params=pltpu.CompilerParams(vmem_limit_bytes=VMEM_LIMIT),
+        cost_estimate=pl.CostEstimate(
+            flops=2 * rows * depth * columns,
+            bytes_accessed=2 * (rows * depth + depth * columns + rows * columns),
+            transcendentals=0,
+        ),
+    )(place[axis].reshape(1), left, *([right] * len(specs)), *ties)
+
+
+def add_up(refs, index):
+    total = refs[0][index].astype(jnp.float32)
+    for ref in refs[1:]:
+        total = total + ref[index].astype(jnp.float32)
     return total
 
 
-def scatter_dp(first_parts, second_parts, place):
-    def whole(parts):
-        return [
-            part.reshape(RING, PAIR, RING, part.shape[0] // (RING * PAIR * RING), part.shape[1])
-            for part in parts
+def second_stage_kernel(by_rows, here, *refs):
+    by_x, by_y = refs[:RING], refs[RING : 2 * RING]
+    outs_x, outs_y = refs[-2 * RING : -RING], refs[-RING:]
+    lanes = outs_x[0].shape[1] // PAIR
+    for offset in range(RING):
+        next_x = (here[0] + offset) % RING
+        next_y = (here[2] + offset) % RING
+        for z in range(PAIR):
+            for parts, outs, slot in (
+                (by_x, outs_x, z * RING + next_y),
+                (by_y, outs_y, next_x * PAIR + z),
+            ):
+                if by_rows:
+                    outs[offset][z] = add_up(parts, slot).astype(jnp.bfloat16)
+                else:
+                    index = (slice(None), pl.ds(pl.multiple_of(slot * lanes, lanes), lanes))
+                    outs[offset][:, z * lanes : (z + 1) * lanes] = add_up(parts, index).astype(
+                        jnp.bfloat16
+                    )
+
+
+def third_stage_kernel(by_rows, here, *refs):
+    by_x, by_y = refs[:RING], refs[RING : 2 * RING]
+    kept, sent = refs[-2], refs[-1]
+    for out, z in ((kept, here[1]), (sent, (here[1] + 1) % PAIR)):
+        if by_rows:
+            width = by_x[0].shape[-1]
+            out[:, :width] = add_up(by_x, z).astype(jnp.bfloat16)
+            out[:, width:] = add_up(by_y, z).astype(jnp.bfloat16)
+        else:
+            rows, lanes = by_x[0].shape[0], out.shape[1]
+            index = (slice(None), pl.ds(pl.multiple_of(z * lanes, lanes), lanes))
+            out[:rows, :] = add_up(by_x, index).astype(jnp.bfloat16)
+            out[rows:, :] = add_up(by_y, index).astype(jnp.bfloat16)
+
+
+def stage_call(kernel, here, operands, outs, ties):
+    whole = pl.BlockSpec(memory_space=pltpu.VMEM)
+    return pl.pallas_call(
+        kernel,
+        in_specs=[pl.BlockSpec(memory_space=pltpu.SMEM)]
+        + [whole] * len(operands)
+        + [pl.BlockSpec(memory_space=pl.ANY)] * len(ties),
+        out_specs=[whole] * len(outs),
+        out_shape=[jax.ShapeDtypeStruct(shape, jnp.bfloat16) for shape in outs],
+        compiler_params=pltpu.CompilerParams(vmem_limit_bytes=VMEM_LIMIT),
+        cost_estimate=pl.CostEstimate(
+            flops=0,
+            bytes_accessed=2 * sum(part.size for part in operands)
+            + 2 * sum(math.prod(shape) for shape in outs),
+            transcendentals=0,
+        ),
+    )(here, *operands, *ties)
+
+
+def exchange(chunks, axis):
+    return [chunks[0]] + [
+        lax.ppermute(chunks[step], "dp", dp_perm(axis, step)) for step in range(1, len(chunks))
+    ]
+
+
+def finish_sum(by_x, by_y, by_rows, place, ties):
+    here = jnp.stack([place["x"], place["z"], place["y"]])
+    got = exchange(by_x, "x") + exchange(by_y, "y")
+    if by_rows:
+        got = [part.reshape(SLOTS, part.shape[0] // SLOTS, part.shape[1]) for part in got]
+        shapes = [(PAIR,) + got[0].shape[1:], (PAIR,) + got[RING].shape[1:]]
+        last = (got[0].shape[1], got[0].shape[2] + got[RING].shape[2])
+    else:
+        shapes = [
+            (got[0].shape[0], PAIR * got[0].shape[1] // SLOTS),
+            (got[RING].shape[0], PAIR * got[RING].shape[1] // SLOTS),
         ]
-
-    def along(parts, axis):
-        def chunk_of(index):
-            return jnp.concatenate(
-                [
-                    lax.dynamic_index_in_dim(part, index, axis, keepdims=False)
-                    for part in parts
-                ],
-                axis=-1,
-            )
-
-        return chunk_of
-
-    by_x = scatter_stage(along(whole(first_parts), 0), "x", place["x"], RING)
-    by_y = scatter_stage(along(whole(second_parts), 2), "y", place["y"], RING)
-    by_x = by_x.astype(jnp.bfloat16)
-    by_y = by_y.astype(jnp.bfloat16)
-    by_x = scatter_stage(along([by_x], 1), "y", place["y"], RING)
-    by_y = scatter_stage(along([by_y], 0), "x", place["x"], RING)
-    both = jnp.concatenate([by_x, by_y], axis=-1).astype(jnp.bfloat16)
-    return scatter_stage(along([both], 0), "z", place["z"], PAIR)
+        last = (got[0].shape[0] + got[RING].shape[0], got[0].shape[1] // SLOTS)
+    parts = stage_call(
+        functools.partial(second_stage_kernel, by_rows),
+        here,
+        got,
+        [shapes[0]] * RING + [shapes[1]] * RING,
+        ties[0],
+    )
+    got = exchange(parts[:RING], "y") + exchange(parts[RING:], "x")
+    kept, sent = stage_call(
+        functools.partial(third_stage_kernel, by_rows), here, got, [last, last], ties[1]
+    )
+    return kept.astype(jnp.float32) + exchange([kept, sent], "z")[1].astype(jnp.float32)
 
 
 def inverse_rms(values):
@@ -316,6 +542,7 @@
     mid_unit = middle * mid_inv
     mid_factor = norm_gains[2] * (1.0 + per_row(scale_ffn, own_segments))
     ffn_rows = all_of(mid_unit * mid_factor)
+    ffn_rows_t = turned(ffn_rows)
     gate_pre = jnp.dot(ffn_rows, gate_weight, preferred_element_type=jnp.float32)
     up_pre = jnp.dot(ffn_rows, up_weight, preferred_element_type=jnp.float32)
     sigmoid_gate = jax.nn.sigmoid(gate_pre)
@@ -336,24 +563,29 @@
     sum_gate_ffn = segment_sum(grad_out * ffn_unit)
     grad_ffn = all_of(norm_back(grad_out * ffn_factor, ffn_unit, ffn_inv))
     grad_hidden = times_transpose(grad_ffn, down_weight)
-    down_grad = contract_rows(grad_ffn, hidden).astype(jnp.bfloat16)
     grad_gate_b = (
         grad_hidden * up_pre * sigmoid_gate * (1.0 + gate_pre * (1.0 - sigmoid_gate))
     ).astype(jnp.bfloat16)
     grad_up_b = (grad_hidden * silu_gate).astype(jnp.bfloat16)
-    grad_ffn_in = scatter_tensor(
+    grad_ffn_in, sent_ffn = scatter_tensor(
         row_blocks(
             times_transpose(grad_gate_b, gate_weight) + times_transpose(grad_up_b, up_weight)
-        )
-    )
-    gate_grad = contract_rows(ffn_rows, grad_gate_b).astype(jnp.bfloat16)
-    up_grad = contract_rows(ffn_rows, grad_up_b).astype(jnp.bfloat16)
+        ),
+        with_sent=True,
+    )
+    half = hidden.shape[1] // 2
+    grad_ffn_t = turned(grad_ffn)
+    ffn_by_x = row_chunks(
+        [(ffn_rows_t, grad_gate_b), (grad_ffn_t, hidden[:, :half])], "x", place, (sent_ffn,)
+    )
+    ffn_by_y = row_chunks(
+        [(ffn_rows_t, grad_up_b), (grad_ffn_t, hidden[:, half:])], "y", place, (sent_ffn,)
+    )
     sum_scale_ffn = segment_sum(grad_ffn_in * mid_unit)
     grad_middle = grad_out + norm_back(grad_ffn_in * mid_factor, mid_unit, mid_inv)
     sum_gate_attn = segment_sum(grad_middle * attn_unit)
     grad_attn = all_of(norm_back(grad_middle * attn_factor, attn_unit, attn_inv))
     grad_mixed_b = times_transpose(grad_attn, out_weight).astype(jnp.bfloat16)
-    outw_grad = contract_rows(grad_attn, mixed).astype(jnp.bfloat16)
     grad_mixed_b = grad_mixed_b.reshape(length, local_heads, HEAD)
     gate_term = jnp.sum(grad_mixed_b.astype(jnp.float32) * cross_out, axis=(0, 2)) * (
         1.0 - tanh_gate * tanh_gate
@@ -366,9 +598,14 @@
         queries_b, keys_b, values_b, self_mask, self_log, grad_mixed_b, unit_scale
     )
     grad_text_raw, grad_gain_text = text_pull(narrow(text_key_back))
-    textkey_grad = contract_rows(caption_flat, grad_text_raw.astype(jnp.bfloat16))
-    textvalue_grad = contract_rows(
-        caption_flat, text_value_back.reshape(caption_flat.shape[0], -1).astype(jnp.bfloat16)
+    text_by_x = column_chunks(
+        turned(grad_text_raw.astype(jnp.bfloat16)), caption_flat, "x", place
+    )
+    text_by_y = column_chunks(
+        turned(text_value_back.reshape(caption_flat.shape[0], -1).astype(jnp.bfloat16)),
+        caption_flat,
+        "y",
+        place,
     )
     grad_raw_query, grad_raw_key, grad_gain_query, grad_gain_key = prep_pull(
         (narrow(query_self + query_cross), narrow(key_self))
@@ -376,16 +613,21 @@
     grad_query_b = grad_raw_query.astype(jnp.bfloat16)
     grad_key_b = grad_raw_key.astype(jnp.bfloat16)
     grad_value_b = value_self.reshape(length, -1).astype(jnp.bfloat16)
-    grad_attn_in = scatter_tensor(
+    grad_attn_in, sent_attn = scatter_tensor(
         row_blocks(
             times_transpose(grad_query_b, query_weight)
             + times_transpose(grad_key_b, key_weight)
             + times_transpose(grad_value_b, value_weight)
-        )
-    )
-    query_grad = contract_rows(attn_rows, grad_query_b).astype(jnp.bfloat16)
-    key_grad = contract_rows(attn_rows, grad_key_b).astype(jnp.bfloat16)
-    value_grad = contract_rows(attn_rows, grad_value_b).astype(jnp.bfloat16)
+        ),
+        with_sent=True,
+    )
+    attn_rows_t = turned(attn_rows)
+    attn_by_x = row_chunks(
+        [(attn_rows_t, grad_query_b), (attn_rows_t, grad_key_b)], "x", place, (sent_attn,)
+    )
+    attn_by_y = row_chunks(
+        [(attn_rows_t, grad_value_b), (turned(grad_attn), mixed)], "y", place, (sent_attn,)
+    )
     block_inv = inverse_rms(block_f)
     block_unit = block_f * block_inv
     block_factor = norm_gains[0] * (1.0 + per_row(scale_attn, own_segments))
@@ -394,27 +636,22 @@
         grad_middle + norm_back(grad_attn_in * block_factor, block_unit, block_inv)
     ).astype(jnp.bfloat16)
 
-    half = down_grad.shape[1] // 2
-    ffn_group = scatter_dp(
-        [gate_grad, down_grad[:, :half]], [up_grad, down_grad[:, half:]], place
-    )
-    text_group = scatter_dp(
-        [textkey_grad.astype(jnp.bfloat16)], [textvalue_grad.astype(jnp.bfloat16)], place
-    )
-    attn_group = scatter_dp([query_grad, key_grad], [value_grad, outw_grad], place)
-    hidden_cols = gate_grad.shape[1]
+    ffn_group = finish_sum(ffn_by_x, ffn_by_y, True, place, ((text_value_back,), (query_self,)))
+    text_group = finish_sum(text_by_x, text_by_y, False, place, ((attn_by_x[0],), (attn_by_y[0],)))
+    attn_group = finish_sum(attn_by_x, attn_by_y, True, place, ((), ()))
+    hidden_cols = grad_gate_b.shape[1]
     gate_sum = ffn_group[:, :hidden_cols]
     up_sum = ffn_group[:, hidden_cols + half : 2 * hidden_cols + half]
     down_sum = jnp.concatenate(
         [ffn_group[:, hidden_cols : hidden_cols + half], ffn_group[:, 2 * hidden_cols + half :]],
         axis=1,
     ).T
-    head_cols = query_grad.shape[1]
+    head_cols = grad_query_b.shape[1]
     query_sum, key_sum, value_sum, outw_sum = [
         attn_group[:, block * head_cols : (block + 1) * head_cols] for block in range(4)
     ]
-    textkey_sum = text_group[:, :head_cols]
-    textvalue_sum = text_group[:, head_cols:]
+    textkey_sum = text_group[:head_cols].T
+    textvalue_sum = text_group[head_cols:].T
 
     sums = jnp.stack([sum_scale_attn, sum_gate_attn, sum_scale_ffn, sum_gate_ffn])
     own_sum = scatter_tensor([pick(sums, block) for block in order])
@@ -433,7 +670,7 @@
     factor = jnp.where(is_gate, tanh_all, 1.0 + parts_all)
     slope = jnp.where(is_gate, 1.0 - tanh_all * tanh_all, 1.0)
     grad_mod = all_sums * slope * pick(norm_gains, position)
-    ada_rows = acts.shape[1] // (RING * PAIR * RING)
+    ada_rows = acts.shape[1] // BLOCKS
     own_cols = lax.dynamic_slice_in_dim(
         acts.astype(jnp.float32), lax.axis_index("dp") * ada_rows, ada_rows, 1
     )

time: 562 us -> 578 us (1.028)
  waiting for transfers between devices: 208 us -> 123 us
  Pallas kernels: 0 us -> 52.4 us
  other arithmetic: 68 us -> 100 us
  starting transfers between devices: 87.6 us -> 96.4 us
  local copies, waits for them, and re-layouts: 87.3 us -> 95.7 us
    ppermute x39, waiting for transfers between devices: 138 us -> 68.9 us  [exchange(): lax.ppermute(chunks[step], 'dp', dp_perm(axis, step))]
    pallas_call x0 -> x18, Pallas kernels: none -> 52.4 us  [the longest x4 20.4 us: row_chunks(): pl.pallas_call(functools.partial(row_chunk_kernel, len(pairs)), grid_spec...]
    dynamic_slice x28 -> x0, local copies, waits for them, and re-layouts: 29.2 us -> none  [chunk_of(): lax.dynamic_index_in_dim(part, index, axis, keepdims=False)]
    dot_general x9 -> x0, matrix products: 22.2 us -> none  [contract_rows(): lax.dot_general(left, right, (((0,), (0,)), ((), ())), preferred_element_...]
    ppermute x11, waiting for transfers between devices: 46 us -> 29.9 us  [swap_chip(): return lax.ppermute(values, 'tensor', CHIP_SWAP)]
    convert_element_type x0 -> x9, local copies, waits for them, and re-layouts: none -> 12.4 us  [the longest x2 2.78 us: shards(): grad_query_b = grad_raw_query.astype(jnp.bfloat16)]
    unnamed x423 -> x521, local copies, waits for them, and re-layouts: 31.8 us -> 42.6 us
    another operation x1 -> x5, local copies, waits for them, and re-layouts: 0.01 us -> 9.69 us
  transfers between devices with their start and end apart: 81 -> 81, of which waited for: 32 -> 26; matrix products, arithmetic and copies ran while one was open for 28% -> 32% of each run, Pallas kernels for 0% -> 9%
where the time goes in v2:
time: 578 us; the launch traced here: 568 us
  waiting for transfers between devices  123 us (21%)
  other arithmetic  100 us (17%)
  starting transfers between devices  96.4 us (17%)
  matrix products  96.3 us (17%)
  local copies, waits for them, and re-layouts  95.7 us (17%)
  Pallas kernels  52.4 us (9%)
    ppermute x39, waiting for transfers between devices, exchange(): lax.ppermute(chunks[step], 'dp', dp_perm(axis, step))  68.9 us
    ppermute x39, starting transfers between devices, exchange(): lax.ppermute(chunks[step], 'dp', dp_perm(axis, step))  58.5 us
    unnamed x521, local copies, waits for them, and re-layouts  42.6 us
    ppermute x11, waiting for transfers between devices, swap_chip(): return lax.ppermute(values, 'tensor', CHIP_SWAP)  29.9 us
    ppermute x14, starting transfers between devices, gather_dp(): lax.ppermute(block, 'dp', dp_perm(axis, step))  23.1 us
    pallas_call x4, Pallas kernels, row_chunks(): pl.pallas_call(functools.partial(row_chunk_kernel, len(pairs)), grid_spec...  20.4 us
    ppermute x14, waiting for transfers between devices, gather_dp(): lax.ppermute(block, 'dp', dp_perm(axis, step))  19.6 us
    dot_general x7, matrix products, times_transpose(): lax.dot_general(left, right, (((1,), (1,)), ((), ())), preferred_element_...  16.9 us
  transfers between devices with their start and end apart: 81, of which 26 were waited for; matrix products, arithmetic and copies ran while one was open for 32% of the time, Pallas kernels for 9%

profile of v2, /device:TPU:0, one launch (start us, length us, event | category | flops | bytes accessed | tf_op | source)
XLA Modules:
  0.0 568.1 jit_solution(3111618545651856954)
XLA Ops:
  12.1 4.7 copy.206
  16.8 7.5 %multiply_reduce_fusion.6 = (f32[768,6]{0,1:T(8,128)S(1)}, f32[768,6,64]{0,2,1:T(8,128)}) fusion(bf16[768,4096,1]{1,0,2:T(8,128)(2,1)} %bitcast.176, bf16[6,64,4096]{2,1,0:T(8,128)(2,1)} %bitcast.202), kind=kOutput, calls=%fused_computation.100 | convolution fusion | flops 2416504320 | bytes 10635264 | tf_op jit(solution)/shard_map/dot_general | solution.py:512
  26.7 6.4 %convolution_convert_fusion.2 = bf16[768,384]{0,1:T(8,128)(2,1)} fusion(bf16[768,4096]{1,0:T(8,128)(2,1)} %bitcast.177, bf16[4096,384]{1,0:T(8,128)(2,1)S(1)} %copy-done.242), kind=kOutput, calls=%fused_computation.81 | convolution fusion | flops 2416214016 | bytes 10027008 | tf_op jit(solution)/shard_map/dot_general | solution.py:515
  92.3 3.8 fusion.26
  103.5 9.4 %collective-permute-done.7 = bf16[128,1536]{1,0:T(8,128)(2,1)S(1)} collective-permute-done((bf16[128,1536]{1,0:T(8,128)(2,1)S(1)}, bf16[128,1536]{1,0:T(8,128)(2,1)S(1)}, u32[]{:S(2)}, u32[]{:S(2)}) %collective-permute-start.7) | collective-permute-done | bytes 393248 | tf_op jit(solution)/shard_map/ppermute | solution.py:52
  117.3 8.9 %collective-permute-done.9 = bf16[128,1536]{1,0:T(8,128)(2,1)S(1)} collective-permute-done((bf16[128,1536]{1,0:T(8,128)(2,1)S(1)}, bf16[128,1536]{1,0:T(8,128)(2,1)S(1)}, u32[]{:S(2)}, u32[]{:S(2)}) %collective-permute-start.9) | collective-permute-done | bytes 393248 | tf_op jit(solution)/shard_map/ppermute | solution.py:52
  180.1 5.1 multiply_convert_fusion.3
  206.8 5.9 %collective-permute-done.17 = bf16[128,1536]{1,0:T(8,128)(2,1)S(1)} collective-permute-done((bf16[128,1536]{1,0:T(8,128)(2,1)S(1)}, bf16[128,1536]{1,0:T(8,128)(2,1)S(1)}, u32[]{:S(2)}, u32[]{:S(2)}) %collective-permute-start.17) | collective-permute-done | bytes 393248 | tf_op jit(solution)/shard_map/ppermute | solution.py:52
  217.9 5.6 shard_map.313
  229.3 5.4 shard_map.312
  244.2 4.0 multiply_reduce_fusion.1
  248.2 4.8 multiply_convert_fusion.1
  259.8 5.7 %multiply_reduce_fusion = (f32[6,512]{1,0:T(8,128)}, f32[6,512,768]{2,1,0:T(8,128)}) fusion(f32[6,512,768]{2,1,0:T(8,128)S(1)} %bitcast.188, f32[6]{0:T(128)S(1)} %copy-done.228, f32[6,512]{1,0:T(8,128)S(1)} %copy-done.161, bf16[512,6,64]{0,2,1:T(8,128)(2,1)S(1)} %bitcast.194, bf16[768,6,64]{0,2,1:T(8,128)(2,1)S(1)} %bitcast.213), kind=kOutput, calls=%fused_computation.1 | convolution fusion | flops 311424000 | bytes 19882008 | tf_op jit(solution)/shard_map/qhd,khd->hqk/dot_general | solution.py:407
  269.9 10.1 %multiply_convert_fusion = bf16[6,512,768]{2,1,0:T(8,128)(2,1)} fusion(f32[6,512,768]{2,1,0:T(8,128)} %get-tuple-element.332, f32[6,512,768]{2,1,0:T(8,128)} %copy-done.47, f32[6,512]{1,0:T(8,128)S(1)} %copy-done.204, f32[6]{0:T(128)S(1)} %copy-done.228, f32[6,512]{1,0:T(8,128)S(1)} %copy-done.162), kind=kLoop, calls=%fused_computation | loop fusion | flops 11796480 | bytes 23617560 | tf_op jit(solution)/shard_map/convert_element_type | solution.py:416
  280.0 3.9 fusion.100
  295.4 4.1 multiply_reduce_fusion.3
  304.7 4.6 fusion.104
  309.5 7.1 %fusion.18 = (bf16[512,6,64]{2,1,0:T(8,128)(2,1)}, bf16[512,6,64]{2,1,0:T(8,128)(2,1)}) fusion(f32[512,6,64]{2,1,0:T(8,128)S(1)} %copy-done.50, f32[512,6]{1,0:T(8,128)S(1)} %copy-done.126, f32[64]{0:T(128)S(1)} %copy-done.217, f32[512,6]{1,0:T(8,128)S(1)} %copy-done.85, f32[512,6,32]{2,1,0:T(8,128)} %get-tuple-element.274, ...), kind=kLoop, calls=%fused_computation.42 | loop fusion | flops 2752512 | bytes 3981824 | tf_op jit(solution)/shard_map/convert_element_type | solution.py:613
  328.9 8.0 %shard_map.307 = (bf16[384,1024]{1,0:T(8,128)(2,1)S(1)}, bf16[384,1024]{1,0:T(8,128)(2,1)}, bf16[384,1024]{1,0:T(8,128)(2,1)S(1)}, bf16[384,1024]{1,0:T(8,128)(2,1)S(1)}) custom-call(s32[1]{0:T(128)} %bitcast.46.here, bf16[384,768]{1,0:T(8,128)(2,1)S(1)} %copy-done.6, bf16[768,4096]{1,0:T(8,128)(2,1)} %bitcast.178, bf16[768,4096]{1,0:T(8,128)(2,1)} %bitcast.179, ...), custom_call_target="tpu_custom_call" | custom-call | flops 2415919104 | bytes 10027008 | tf_op jit(solution)/shard_map/pallas_call | solution.py:239
  344.9 5.3 shard_map.314
  370.6 6.2 %collective-permute-done.74.refs_1_ = bf16[2,48,1536]{2,1,0:T(8,128)(2,1)S(1)} collective-permute-done((bf16[2,48,1536]{2,1,0:T(8,128)(2,1)S(1)}, bf16[2,48,1536]{2,1,0:T(8,128)(2,1)S(1)}, u32[]{:S(2)}, u32[]{:S(2)}) %collective-permute-start.74) | collective-permute-done | bytes 294944 | tf_op jit(solution)/shard_map/ppermute | solution.py:327
  384.7 4.2 collective-permute-done.77.refs_5_
  399.7 5.5 shard_map.305
  410.2 4.8 shard_map.299
  415.8 7.6 %collective-permute-done.60.refs_7_ = bf16[384,1024]{1,0:T(8,128)(2,1)S(1)} collective-permute-done((bf16[384,1024]{1,0:T(8,128)(2,1)S(1)}, bf16[384,1024]{1,0:T(8,128)(2,1)S(1)}, u32[]{:S(2)}, u32[]{:S(2)}) %collective-permute-start.60) | collective-permute-done | bytes 786464 | tf_op jit(solution)/shard_map/ppermute | solution.py:327
  423.4 17.5 %collective-permute-done.55.refs_1_ = bf16[384,1024]{1,0:T(8,128)(2,1)S(1)} collective-permute-done((bf16[384,1024]{1,0:T(8,128)(2,1)S(1)}, bf16[384,1024]{1,0:T(8,128)(2,1)S(1)}, u32[]{:S(2)}, u32[]{:S(2)}) %collective-permute-start.55) | collective-permute-done | bytes 786464 | tf_op jit(solution)/shard_map/ppermute | solution.py:327
  441.8 4.0 shard_map.308
  451.5 4.9 collective-permute-done.61.refs_1_
  461.7 4.6 shard_map.301
  484.6 10.0 %collective-permute-done.33 = f32[2,4,1536]{2,1,0:T(4,128)S(1)} collective-permute-done((f32[2,4,1536]{2,1,0:T(4,128)S(1)}, f32[2,4,1536]{2,1,0:T(4,128)S(1)}, u32[]{:S(2)}, u32[]{:S(2)}) %collective-permute-start.33) | collective-permute-done | bytes 49184 | tf_op jit(solution)/shard_map/ppermute | solution.py:93
  505.2 5.0 collective-permute-done.47
  510.5 16.0 %collective-permute-done.42 = bf16[384,768]{1,0:T(8,128)(2,1)S(1)} collective-permute-done((bf16[384,768]{1,0:T(8,128)(2,1)S(1)}, bf16[384,768]{1,0:T(8,128)(2,1)S(1)}, u32[]{:S(2)}, u32[]{:S(2)}) %collective-permute-start.42) | collective-permute-done | bytes 589856 | tf_op jit(solution)/shard_map/ppermute | solution.py:327
  (866 shorter events, 353.6 us)
Async XLA Ops:
  3.9 31.7 %collective-permute-start.1 = (f32[3,1536]{1,0:T(4,128)}, f32[3,1536]{1,0:T(4,128)}, u32[]{:S(2)}, u32[]{:S(2)}) collective-permute-start(f32[3,1536]{1,0:T(4,128)} %fusion.81), channel_id=1, source_target_pairs={{0,2},{2,0},{1,3},{3,1},{4,6},{6,4},{5,7},{7,5},{8,10},{10,8},{9,1... | collective-permute-start | bytes 55304 | tf_op jit(solution)/shard_map/ppermute | solution.py:52
  5.9 33.1 %collective-permute-start = (f32[3,1536]{1,0:T(4,128)}, f32[3,1536]{1,0:T(4,128)}, u32[]{:S(2)}, u32[]{:S(2)}) collective-permute-start(f32[3,1536]{1,0:T(4,128)} %fusion.81), channel_id=1, source_target_pairs={{0,1},{1,0},{2,3},{3,2},{4,5},{5,4},{6,7},{7,6},{8,9},{9,8},{10,11... | collective-permute-start | bytes 55304 | tf_op jit(solution)/shard_map/ppermute | solution.py:48
  5.9 34.7 %collective-permute-start.3 = (bf16[128,1536]{1,0:T(8,128)(2,1)S(1)}, bf16[128,1536]{1,0:T(8,128)(2,1)}, u32[]{:S(2)}, u32[]{:S(2)}) collective-permute-start(bf16[128,1536]{1,0:T(8,128)(2,1)S(1)} %copy-done.72), channel_id=1, source_target_pairs={{0,1},{1,0},{2,3},{3,2},{4,5},{5,4},{6,7},{7,6},{8,9},{9,8},{10,11... | collective-permute-start | bytes 1179656 | tf_op jit(solution)/shard_map/ppermute | solution.py:48
  6.4 29.1 %collective-permute-start.4 = (bf16[128,1536]{1,0:T(8,128)(2,1)S(1)}, bf16[128,1536]{1,0:T(8,128)(2,1)}, u32[]{:S(2)}, u32[]{:S(2)}) collective-permute-start(bf16[128,1536]{1,0:T(8,128)(2,1)S(1)} %copy-done.72), channel_id=1, source_target_pairs={{0,2},{2,0},{1,3},{3,1},{4,6},{6,4},{5,7},{7,5},{8,10},{10,8},{9,1... | collective-permute-start | bytes 1179656 | tf_op jit(solution)/shard_map/ppermute | solution.py:52
  216.7 18.1 %collective-permute-start.19 = (bf16[128,1536]{1,0:T(8,128)(2,1)S(1)}, bf16[128,1536]{1,0:T(8,128)(2,1)S(1)}, u32[]{:S(2)}, u32[]{:S(2)}) collective-permute-start(bf16[128,1536]{1,0:T(8,128)(2,1)S(1)} %multiply_convert_fusion.7), channel_id=1, source_target_pairs={{0,2},{2,0},{1,3},{3,1},{4,6},{6,4},{5,7},{7,5},{8,10},{10,8},{9,1... | collective-permute-start | bytes 1179656 | tf_op jit(solution)/shard_map/ppermute | solution.py:52
  224.4 92.2 %collective-permute-start.71 = (bf16[384,1536]{1,0:T(8,128)(2,1)}, bf16[384,1536]{1,0:T(8,128)(2,1)}, u32[]{:S(2)}, u32[]{:S(2)}) collective-permute-start(bf16[384,1536]{1,0:T(8,128)(2,1)} %get-tuple-element.110), channel_id=1, source_target_pairs={{0,4},{4,8},{8,12},{12,0},{16,20},{20,24},{24,28},{28,16},{32,36},... | collective-permute-start | bytes 3538952 | tf_op jit(solution)/shard_map/ppermute | solution.py:327
  226.3 117.6 %collective-permute-start.72 = (bf16[384,1536]{1,0:T(8,128)(2,1)}, bf16[384,1536]{1,0:T(8,128)(2,1)}, u32[]{:S(2)}, u32[]{:S(2)}) collective-permute-start(bf16[384,1536]{1,0:T(8,128)(2,1)} %get-tuple-element.111), channel_id=1, source_target_pairs={{0,8},{4,12},{8,0},{12,4},{16,24},{20,28},{24,16},{28,20},{32,40},... | collective-permute-start | bytes 3538952 | tf_op jit(solution)/shard_map/ppermute | solution.py:327
  228.2 116.7 %collective-permute-start.73 = (bf16[384,1536]{1,0:T(8,128)(2,1)}, bf16[384,1536]{1,0:T(8,128)(2,1)}, u32[]{:S(2)}, u32[]{:S(2)}) collective-permute-start(bf16[384,1536]{1,0:T(8,128)(2,1)} %get-tuple-element.112), channel_id=1, source_target_pairs={{0,12},{4,0},{8,4},{12,8},{16,28},{20,16},{24,20},{28,24},{32,44},... | collective-permute-start | bytes 3538952 | tf_op jit(solution)/shard_map/ppermute | solution.py:327
  239.1 105.8 %collective-permute-start.68 = (bf16[384,1536]{1,0:T(8,128)(2,1)}, bf16[384,1536]{1,0:T(8,128)(2,1)}, u32[]{:S(2)}, u32[]{:S(2)}) collective-permute-start(bf16[384,1536]{1,0:T(8,128)(2,1)} %get-tuple-element.106), channel_id=1, source_target_pairs={{0,32},{4,36},{8,40},{12,44},{16,48},{20,52},{24,56},{28,60},{32,6... | collective-permute-start | bytes 3538952 | tf_op jit(solution)/shard_map/ppermute | solution.py:327
  239.1 105.7 %collective-permute-start.69 = (bf16[384,1536]{1,0:T(8,128)(2,1)}, bf16[384,1536]{1,0:T(8,128)(2,1)}, u32[]{:S(2)}, u32[]{:S(2)}) collective-permute-start(bf16[384,1536]{1,0:T(8,128)(2,1)} %get-tuple-element.107), channel_id=1, source_target_pairs={{0,64},{4,68},{8,72},{12,76},{16,80},{20,84},{24,88},{28,92},{32,9... | collective-permute-start | bytes 3538952 | tf_op jit(solution)/shard_map/ppermute | solution.py:327
  316.6 28.3 %collective-permute-start.70 = (bf16[384,1536]{1,0:T(8,128)(2,1)}, bf16[384,1536]{1,0:T(8,128)(2,1)}, u32[]{:S(2)}, u32[]{:S(2)}) collective-permute-start(bf16[384,1536]{1,0:T(8,128)(2,1)} %get-tuple-element.108), channel_id=1, source_target_pairs={{0,96},{4,100},{8,104},{12,108},{16,112},{20,116},{24,120},{28,124... | collective-permute-start | bytes 3538952 | tf_op jit(solution)/shard_map/ppermute | solution.py:327
  343.9 61.5 %collective-permute-start.58 = (bf16[384,1024]{1,0:T(8,128)(2,1)}, bf16[384,1024]{1,0:T(8,128)(2,1)}, u32[]{:S(2)}, u32[]{:S(2)}) collective-permute-start(bf16[384,1024]{1,0:T(8,128)(2,1)} %get-tuple-element.92), channel_id=1, source_target_pairs={{0,4},{4,8},{8,12},{12,0},{16,20},{20,24},{24,28},{28,16},{32,36},... | collective-permute-start | bytes 2359304 | tf_op jit(solution)/shard_map/ppermute | solution.py:327
  352.4 24.5 %collective-permute-start.74 = (bf16[2,48,1536]{2,1,0:T(8,128)(2,1)S(1)}, bf16[2,48,1536]{2,1,0:T(8,128)(2,1)S(1)}, u32[]{:S(2)}, u32[]{:S(2)}) collective-permute-start(bf16[2,48,1536]{2,1,0:T(8,128)(2,1)S(1)} %get-tuple-element.114), channel_id=1, source_target_pairs={{0,4},{4,8},{8,12},{12,0},{16,20},{20,24},{24,28},{28,16},{32,36},... | collective-permute-start | bytes 884744 | tf_op jit(solution)/shard_map/ppermute | solution.py:327
  352.7 24.3 %collective-permute-start.75 = (bf16[2,48,1536]{2,1,0:T(8,128)(2,1)S(1)}, bf16[2,48,1536]{2,1,0:T(8,128)(2,1)S(1)}, u32[]{:S(2)}, u32[]{:S(2)}) collective-permute-start(bf16[2,48,1536]{2,1,0:T(8,128)(2,1)S(1)} %get-tuple-element.115), channel_id=1, source_target_pairs={{0,8},{4,12},{8,0},{12,4},{16,24},{20,28},{24,16},{28,20},{32,40},... | collective-permute-start | bytes 884744 | tf_op jit(solution)/shard_map/ppermute | solution.py:327
  356.2 22.7 %collective-permute-start.76 = (bf16[2,48,1536]{2,1,0:T(8,128)(2,1)}, bf16[2,48,1536]{2,1,0:T(8,128)(2,1)S(1)}, u32[]{:S(2)}, u32[]{:S(2)}) collective-permute-start(bf16[2,48,1536]{2,1,0:T(8,128)(2,1)} %get-tuple-element.116), channel_id=1, source_target_pairs={{0,12},{4,0},{8,4},{12,8},{16,28},{20,16},{24,20},{28,24},{32,44},... | collective-permute-start | bytes 884744 | tf_op jit(solution)/shard_map/ppermute | solution.py:327
  370.4 36.6 %collective-permute-start.21 = (bf16[256,1536]{1,0:T(8,128)(2,1)}, bf16[256,1536]{1,0:T(8,128)(2,1)S(1)}, u32[]{:S(2)}, u32[]{:S(2)}) collective-permute-start(bf16[256,1536]{1,0:T(8,128)(2,1)} %pad_maximum_fusion.7), channel_id=1, source_target_pairs={{0,1},{1,0},{2,3},{3,2},{4,5},{5,4},{6,7},{7,6},{8,9},{9,8},{10,11... | collective-permute-start | bytes 2359304 | tf_op jit(solution)/shard_map/ppermute | solution.py:48
  388.9 26.1 %collective-permute-start.59 = (bf16[384,1024]{1,0:T(8,128)(2,1)S(1)}, bf16[384,1024]{1,0:T(8,128)(2,1)S(1)}, u32[]{:S(2)}, u32[]{:S(2)}) collective-permute-start(bf16[384,1024]{1,0:T(8,128)(2,1)S(1)} %copy-done.36), channel_id=1, source_target_pairs={{0,8},{4,12},{8,0},{12,4},{16,24},{20,28},{24,16},{28,20},{32,40},... | collective-permute-start | bytes 2359304 | tf_op jit(solution)/shard_map/ppermute | solution.py:327
  388.9 34.5 %collective-permute-start.60 = (bf16[384,1024]{1,0:T(8,128)(2,1)S(1)}, bf16[384,1024]{1,0:T(8,128)(2,1)S(1)}, u32[]{:S(2)}, u32[]{:S(2)}) collective-permute-start(bf16[384,1024]{1,0:T(8,128)(2,1)S(1)} %copy-done.34), channel_id=1, source_target_pairs={{0,12},{4,0},{8,4},{12,8},{16,28},{20,16},{24,20},{28,24},{32,44},... | collective-permute-start | bytes 2359304 | tf_op jit(solution)/shard_map/ppermute | solution.py:327
  405.3 35.6 %collective-permute-start.55 = (bf16[384,1024]{1,0:T(8,128)(2,1)S(1)}, bf16[384,1024]{1,0:T(8,128)(2,1)S(1)}, u32[]{:S(2)}, u32[]{:S(2)}) collective-permute-start(bf16[384,1024]{1,0:T(8,128)(2,1)S(1)} %get-tuple-element.88), channel_id=1, source_target_pairs={{0,32},{4,36},{8,40},{12,44},{16,48},{20,52},{24,56},{28,60},{32,6... | collective-permute-start | bytes 2359304 | tf_op jit(solution)/shard_map/ppermute | solution.py:327
  405.4 35.5 %collective-permute-start.56 = (bf16[384,1024]{1,0:T(8,128)(2,1)S(1)}, bf16[384,1024]{1,0:T(8,128)(2,1)S(1)}, u32[]{:S(2)}, u32[]{:S(2)}) collective-permute-start(bf16[384,1024]{1,0:T(8,128)(2,1)S(1)} %get-tuple-element.89), channel_id=1, source_target_pairs={{0,64},{4,68},{8,72},{12,76},{16,80},{20,84},{24,88},{28,92},{32,9... | collective-permute-start | bytes 2359304 | tf_op jit(solution)/shard_map/ppermute | solution.py:327
  407.0 34.6 %collective-permute-start.57 = (bf16[384,1024]{1,0:T(8,128)(2,1)S(1)}, bf16[384,1024]{1,0:T(8,128)(2,1)}, u32[]{:S(2)}, u32[]{:S(2)}) collective-permute-start(bf16[384,1024]{1,0:T(8,128)(2,1)S(1)} %get-tuple-element.90), channel_id=1, source_target_pairs={{0,96},{4,100},{8,104},{12,108},{16,112},{20,116},{24,120},{28,124... | collective-permute-start | bytes 2359304 | tf_op jit(solution)/shard_map/ppermute | solution.py:327
  415.0 55.5 %collective-permute-start.22 = (bf16[128,1536]{1,0:T(8,128)(2,1)S(1)}, bf16[128,1536]{1,0:T(8,128)(2,1)S(1)}, u32[]{:S(2)}, u32[]{:S(2)}) collective-permute-start(bf16[128,1536]{1,0:T(8,128)(2,1)S(1)} %add_convert_fusion.2.refs_4_), channel_id=1, source_target_pairs={{0,2},{2,0},{1,3},{3,1},{4,6},{6,4},{5,7},{7,5},{8,10},{10,8},{9,1... | collective-permute-start | bytes 1179656 | tf_op jit(solution)/shard_map/ppermute | solution.py:52
  447.7 18.7 %collective-permute-start.63 = (bf16[384,256]{1,0:T(8,128)(2,1)S(1)}, bf16[384,256]{1,0:T(8,128)(2,1)S(1)}, u32[]{:S(2)}, u32[]{:S(2)}) collective-permute-start(bf16[384,256]{1,0:T(8,128)(2,1)S(1)} %get-tuple-element.98), channel_id=1, source_target_pairs={{0,12},{4,0},{8,4},{12,8},{16,28},{20,16},{24,20},{28,24},{32,44},... | collective-permute-start | bytes 589832 | tf_op jit(solution)/shard_map/ppermute | solution.py:327
  466.4 36.4 %collective-permute-start.45 = (bf16[384,768]{1,0:T(8,128)(2,1)S(1)}, bf16[384,768]{1,0:T(8,128)(2,1)S(1)}, u32[]{:S(2)}, u32[]{:S(2)}) collective-permute-start(bf16[384,768]{1,0:T(8,128)(2,1)S(1)} %get-tuple-element.74), channel_id=1, source_target_pairs={{0,4},{4,8},{8,12},{12,0},{16,20},{20,24},{24,28},{28,16},{32,36},... | collective-permute-start | bytes 1769480 | tf_op jit(solution)/shard_map/ppermute | solution.py:327
  466.5 37.3 %collective-permute-start.46 = (bf16[384,768]{1,0:T(8,128)(2,1)S(1)}, bf16[384,768]{1,0:T(8,128)(2,1)S(1)}, u32[]{:S(2)}, u32[]{:S(2)}) collective-permute-start(bf16[384,768]{1,0:T(8,128)(2,1)S(1)} %get-tuple-element.75), channel_id=1, source_target_pairs={{0,8},{4,12},{8,0},{12,4},{16,24},{20,28},{24,16},{28,20},{32,40},... | collective-permute-start | bytes 1769480 | tf_op jit(solution)/shard_map/ppermute | solution.py:327
  469.8 25.4 %collective-permute-start.67 = (bf16[768,128]{1,0:T(8,128)(2,1)S(1)}, bf16[768,128]{1,0:T(8,128)(2,1)S(1)}, u32[]{:S(2)}, u32[]{:S(2)}) collective-permute-start(bf16[768,128]{1,0:T(8,128)(2,1)S(1)} %get-tuple-element.104), channel_id=1, source_target_pairs={{0,16},{4,20},{8,24},{12,28},{16,0},{20,4},{24,8},{28,12},{32,48},... | collective-permute-start | bytes 589832 | tf_op jit(solution)/shard_map/ppermute | solution.py:327
  496.5 30.1 %collective-permute-start.42 = (bf16[384,768]{1,0:T(8,128)(2,1)S(1)}, bf16[384,768]{1,0:T(8,128)(2,1)S(1)}, u32[]{:S(2)}, u32[]{:S(2)}) collective-permute-start(bf16[384,768]{1,0:T(8,128)(2,1)S(1)} %get-tuple-element.70), channel_id=1, source_target_pairs={{0,32},{4,36},{8,40},{12,44},{16,48},{20,52},{24,56},{28,60},{32,6... | collective-permute-start | bytes 1769480 | tf_op jit(solution)/shard_map/ppermute | solution.py:327
  500.2 28.1 %collective-permute-start.43 = (bf16[384,768]{1,0:T(8,128)(2,1)S(1)}, bf16[384,768]{1,0:T(8,128)(2,1)S(1)}, u32[]{:S(2)}, u32[]{:S(2)}) collective-permute-start(bf16[384,768]{1,0:T(8,128)(2,1)S(1)} %get-tuple-element.71), channel_id=1, source_target_pairs={{0,64},{4,68},{8,72},{12,76},{16,80},{20,84},{24,88},{28,92},{32,9... | collective-permute-start | bytes 1769480 | tf_op jit(solution)/shard_map/ppermute | solution.py:327
  502.8 25.4 %collective-permute-start.44 = (bf16[384,768]{1,0:T(8,128)(2,1)S(1)}, bf16[384,768]{1,0:T(8,128)(2,1)S(1)}, u32[]{:S(2)}, u32[]{:S(2)}) collective-permute-start(bf16[384,768]{1,0:T(8,128)(2,1)S(1)} %get-tuple-element.72), channel_id=1, source_target_pairs={{0,96},{4,100},{8,104},{12,108},{16,112},{20,116},{24,120},{28,124... | collective-permute-start | bytes 1769480 | tf_op jit(solution)/shard_map/ppermute | solution.py:327
  503.8 31.2 %collective-permute-start.36 = (f32[8,4,1536]{2,1,0:T(4,128)S(1)}, f32[8,4,1536]{2,1,0:T(4,128)S(1)}, u32[]{:S(2)}, u32[]{:S(2)}) collective-permute-start(f32[8,4,1536]{2,1,0:T(4,128)S(1)} %get-tuple-element.289), channel_id=1, source_target_pairs={{0,32},{4,36},{8,40},{12,44},{16,48},{20,52},{24,56},{28,60},{32,6... | collective-permute-start | bytes 589832 | tf_op jit(solution)/shard_map/ppermute | solution.py:93
  510.2 24.8 %collective-permute-start.38 = (f32[8,4,1536]{2,1,0:T(4,128)S(1)}, f32[8,4,1536]{2,1,0:T(4,128)S(1)}, u32[]{:S(2)}, u32[]{:S(2)}) collective-permute-start(f32[8,4,1536]{2,1,0:T(4,128)S(1)} %get-tuple-element.289), channel_id=1, source_target_pairs={{0,96},{4,100},{8,104},{12,108},{16,112},{20,116},{24,120},{28,124... | collective-permute-start | bytes 589832 | tf_op jit(solution)/shard_map/ppermute | solution.py:93
  531.8 17.7 %collective-permute-start.49 = (bf16[2,48,768]{2,1,0:T(8,128)(2,1)S(1)}, bf16[2,48,768]{2,1,0:T(8,128)(2,1)S(1)}, u32[]{:S(2)}, u32[]{:S(2)}) collective-permute-start(bf16[2,48,768]{2,1,0:T(8,128)(2,1)S(1)} %get-tuple-element.79), channel_id=1, source_target_pairs={{0,8},{4,12},{8,0},{12,4},{16,24},{20,28},{24,16},{28,20},{32,40},... | collective-permute-start | bytes 442376 | tf_op jit(solution)/shard_map/ppermute | solution.py:327
  (302 other events, 2235.4 us)
